TPU v7x, 128 devices: a whole 4x4x4 slice. The times are simulated.
128 devices in a mesh: lat: 8 (over y, core), lon: 16 (over z, x).
Axes of the slice: x: 4, y: 4, z: 4, core: 2. Of those that a mesh axis runs over, the one named last changes fastest.
Arguments:
- latents: bfloat16 [131072, 512], P(('lat', 'lon')), may hold values from -6 to 6
- d_out: bfloat16 [131072, 512], P(('lat', 'lon')), may hold values from -6 to 6
- observations: bfloat16 [4096, 8, 256], P(('lat', 'lon')), may hold values from -6 to 6
- obs_bias: bfloat16 [4096, 8], P(('lat', 'lon')), may hold values from -2 to 258
- footprint: int32 [4096, 4], P(('lat', 'lon')), may hold values from 0 to 127, all different within a row; in each aligned block of 32 rows (0 to 31, 32 to 63, ...) at most 2 rows name the same one
- obs_cell: int32 [4096, 4, 8], P(('lat', 'lon')), may hold values from 0 to 8
- w_obs: bfloat16 [256, 512], replicated, may hold values from -0.375 to 0.375
- w_kv: bfloat16 [512, 1024], replicated, may hold values from -0.25 to 0.25
- w_q: bfloat16 [512, 512], replicated, may hold values from -0.25 to 0.25
- w_o: bfloat16 [512, 512], replicated, may hold values from -0.25 to 0.25
Outputs:
- updated: bfloat16 [131072, 512], P(('lat', 'lon'))
- d_latents: bfloat16 [131072, 512], P(('lat', 'lon'))
- grad_w_obs: float32 [256, 512], replicated
- grad_w_kv: float32 [512, 1024], replicated
- grad_w_q: float32 [512, 512], replicated
- grad_w_o: float32 [512, 512], replicated
Inputs may be any that keep to these rules, and one draw needn't show every extreme that they name: `footprint`: A block's 4 tiles are distinct. Among the rows of one device no tile is named more than 2 times, a bound that some block reaches. `obs_cell`: the value 8 marks an observation that falls outside that footprint tile.
All inputs are finite; a program needn't handle non-finite values.
Results may differ from a plain program's by a relative error of at most 0.0098.
Values may be sent and summed in bfloat16 or wider, within the bound.
A program may use at most 128 MiB of HBM per device.

v0:
```python
import math

import jax
import jax.numpy as jnp
from jax import lax
from jax.sharding import PartitionSpec as P

HEADS = 8
GROUPS = 8


def gelu_value(x):
    return 0.5 * x * (1.0 + jax.scipy.special.erf(x / math.sqrt(2.0)))


def gelu_slope(x):
    return 0.5 * (1.0 + jax.scipy.special.erf(x / math.sqrt(2.0))) + x * jnp.exp(
        -0.5 * x * x
    ) / math.sqrt(2.0 * math.pi)


def slot_ranks(foot_local, devices):
    flat = foot_local.reshape(-1)
    onehot = (flat[:, None] == jnp.arange(devices, dtype=jnp.int32)[None, :]).astype(jnp.int32)
    running = jnp.cumsum(onehot, axis=0)
    rank = jnp.sum(running * onehot, axis=1) - 1
    return (flat, rank)


def split_heads(x):
    return x.reshape(x.shape[0], HEADS, -1).transpose(1, 0, 2)


def merge_heads(x):
    return x.transpose(1, 0, 2).reshape(x.shape[1], -1)


def slot_grads(rows_s, pre_s, enc_s, dkeyval, w_kv):
    grad_kv = jnp.dot(enc_s.T, dkeyval, preferred_element_type=jnp.float32)
    d_enc = jnp.dot(dkeyval, w_kv.T, preferred_element_type=jnp.float32)
    d_pre = (d_enc * gelu_slope(pre_s)).astype(jnp.bfloat16)
    grad_obs = jnp.dot(rows_s.T, d_pre, preferred_element_type=jnp.float32)
    return (grad_obs, grad_kv)


def attend(lat, dout, keyval, cells, bias, w_q, w_o):
    q_rows = lat.shape[0]
    width = w_q.shape[0]
    scale = 1.0 / math.sqrt(width // HEADS)
    query = jnp.dot(lat, w_q, preferred_element_type=jnp.float32).astype(jnp.bfloat16)
    back = jnp.dot(dout, w_o.T, preferred_element_type=jnp.float32).astype(jnp.bfloat16)
    group = jnp.arange(q_rows, dtype=jnp.int32) // (q_rows // GROUPS)
    visible = group[:, None] == cells[None, :]

    def per_head(inputs):
        qh, kh, vh, dh = inputs
        score = jnp.dot(qh, kh.T, preferred_element_type=jnp.float32) * scale + bias[None, :]
        top = jnp.maximum(jnp.max(jnp.where(visible, score, -jnp.inf), axis=1), 0.0)
        expd = jnp.where(visible, jnp.exp(jnp.where(visible, score, 0.0) - top[:, None]), 0.0)
        denom = jnp.exp(-top) + jnp.sum(expd, axis=1)
        weights = expd / denom[:, None]
        weights_b = weights.astype(jnp.bfloat16)
        attn_h = jnp.dot(weights_b, vh, preferred_element_type=jnp.float32)
        dprob = jnp.dot(dh, vh.T, preferred_element_type=jnp.float32)
        delta = jnp.sum(weights * dprob, axis=1, keepdims=True)
        dscore = (weights * (dprob - delta)).astype(jnp.bfloat16)
        dq_h = jnp.dot(dscore, kh, preferred_element_type=jnp.float32) * scale
        dk_h = jnp.dot(dscore.T, qh, preferred_element_type=jnp.float32) * scale
        dv_h = jnp.dot(weights_b.T, dh, preferred_element_type=jnp.float32)
        return (attn_h, dq_h, dk_h, dv_h)

    heads_out = lax.map(
        per_head,
        (
            split_heads(query),
            split_heads(keyval[:, :width]),
            split_heads(keyval[:, width:]),
            split_heads(back),
        ),
    )
    attn = merge_heads(heads_out[0]).astype(jnp.bfloat16)
    updated = (
        lat.astype(jnp.float32) + jnp.dot(attn, w_o, preferred_element_type=jnp.float32)
    ).astype(jnp.bfloat16)
    grad_o = jnp.dot(attn.T, dout, preferred_element_type=jnp.float32)
    dquery = merge_heads(heads_out[1]).astype(jnp.bfloat16)
    grad_q = jnp.dot(lat.T, dquery, preferred_element_type=jnp.float32)
    d_lat = (
        dout.astype(jnp.float32) + jnp.dot(dquery, w_q.T, preferred_element_type=jnp.float32)
    ).astype(jnp.bfloat16)
    dkeyval = jnp.concatenate(
        [merge_heads(heads_out[2]), merge_heads(heads_out[3])], axis=1
    ).astype(jnp.bfloat16)
    return (updated, d_lat, dkeyval, grad_q, grad_o)


def send_keyval(payload, cells_sent, bias_sent):
    return (
        lax.all_to_all(payload, ("lat", "lon"), split_axis=0, concat_axis=0, tiled=True),
        lax.all_to_all(cells_sent, ("lat", "lon"), split_axis=0, concat_axis=0, tiled=True),
        lax.all_to_all(bias_sent, ("lat", "lon"), split_axis=0, concat_axis=0, tiled=True),
    )


def return_slots(grads):
    return lax.all_to_all(grads, ("lat", "lon"), split_axis=0, concat_axis=0, tiled=True)


def body(latents, d_out, observations, obs_bias, footprint, obs_cell, w_obs, w_kv, w_q, w_o):
    devices = lax.axis_size(("lat", "lon"))
    blocks, obs_rows, channels = observations.shape
    width = w_q.shape[0]
    foot_n = footprint.shape[1]
    pairs = blocks * foot_n
    cap = max(2, 2 * pairs // devices)
    slots = devices * cap
    flat, rank = slot_ranks(footprint, devices)
    target = flat * cap + rank
    placing = (target[None, :] == jnp.arange(slots, dtype=jnp.int32)[:, None]).astype(jnp.float32)
    pair_block = jnp.arange(pairs, dtype=jnp.int32) // foot_n
    by_block = (pair_block[:, None] == jnp.arange(blocks, dtype=jnp.int32)[None, :]).astype(
        jnp.float32
    )
    select_f = jnp.dot(placing, by_block, precision=lax.Precision.HIGHEST)
    select = select_f.astype(jnp.bfloat16)
    filled = jnp.sum(placing, axis=1, keepdims=True)
    cells_pairs = obs_cell.reshape(pairs, obs_rows).astype(jnp.float32)
    cells_sent = (
        jnp.dot(placing, cells_pairs, precision=lax.Precision.HIGHEST) + GROUPS * (1.0 - filled)
    ).astype(jnp.bfloat16)
    bias_sent = jnp.dot(select, obs_bias, preferred_element_type=jnp.float32).astype(jnp.bfloat16)
    block_rows = observations.reshape(blocks, obs_rows * channels)
    rows = observations.reshape(blocks * obs_rows, channels)
    pre = jnp.dot(rows, w_obs, preferred_element_type=jnp.float32)
    enc = gelu_value(pre).astype(jnp.bfloat16)
    keyval = jnp.dot(enc, w_kv, preferred_element_type=jnp.float32).astype(jnp.bfloat16)
    keyval = keyval.reshape(blocks, obs_rows * 2 * width)
    payload = jnp.dot(select, keyval, preferred_element_type=jnp.float32).astype(jnp.bfloat16)
    got_kv, got_cells, got_bias = send_keyval(payload, cells_sent, bias_sent)
    keys = got_kv.reshape(slots * obs_rows, 2 * width)
    cells = got_cells.astype(jnp.float32).astype(jnp.int32).reshape(-1)
    bias = got_bias.astype(jnp.float32).reshape(-1)
    updated, d_lat, dkeyval, grad_q, grad_o = attend(latents, d_out, keys, cells, bias, w_q, w_o)
    returned = return_slots(dkeyval.reshape(slots, obs_rows * 2 * width))
    rows_s = jnp.dot(select, block_rows, preferred_element_type=jnp.float32).astype(jnp.bfloat16)
    rows_s = rows_s.reshape(slots * obs_rows, channels)
    pre_s = jnp.dot(
        select_f, pre.reshape(blocks, obs_rows * width), precision=lax.Precision.HIGHEST
    )
    pre_s = pre_s.reshape(slots * obs_rows, width)
    enc_s = jnp.dot(
        select, enc.reshape(blocks, obs_rows * width), preferred_element_type=jnp.float32
    ).astype(jnp.bfloat16)
    enc_s = enc_s.reshape(slots * obs_rows, width)
    grad_obs, grad_kv = slot_grads(
        rows_s, pre_s, enc_s, returned.reshape(slots * obs_rows, 2 * width), w_kv
    )
    sums = lax.psum((grad_obs, grad_kv, grad_q, grad_o), ("lat", "lon"))
    return (updated, d_lat, sums[0], sums[1], sums[2], sums[3])


def solution(mesh):
    placed = (
        P(("lat", "lon"), None),
        P(("lat", "lon"), None),
        P(("lat", "lon"), None, None),
        P(("lat", "lon"), None),
        P(("lat", "lon"), None),
        P(("lat", "lon"), None, None),
        P(),
        P(),
        P(),
        P(),
    )
    return jax.shard_map(
        body,
        mesh=mesh,
        in_specs=placed,
        out_specs=(P(("lat", "lon"), None), P(("lat", "lon"), None), P(), P(), P(), P()),
        check_vma=False,
    )
```

profile of v0, /device:TPU:1, one launch (start us, length us, event | category | flops | bytes accessed | tf_op | source)
XLA Modules:
  0.0 689.2 jit_solution(3708356820598312037)
XLA Ops:
  11.0 11.5 %all-to-all-start.1 = ((bf16[128,2,8]{2,1,0:T(2,128)(2,1)}), bf16[128,2,8]{2,1,0:T(2,128)(2,1)S(1)}, u32[]{:S(2)}, u32[]{:S(2)}) async-start(bf16[128,2,8]{2,1,0:T(2,128)(2,1)} %bitcast.5), calls=%async_computation.1 | async-start | bytes 131072 | tf_op jit(solution)/shard_map/all_to_all | solution.py:101
  32.2 5.4 all-to-all-start.2
  40.9 7.7 %all_to_all.22 = bf16[128,2,8192]{2,1,0:T(2,128)(2,1)} reshape(bf16[256,8192]{1,0:T(8,128)(2,1)} %convolution_convert_fusion) | data formatting | bytes 8388608 | tf_op jit(solution)/shard_map/all_to_all | solution.py:99
  48.6 10.2 %all-to-all-start = ((bf16[128,2,8192]{2,1,0:T(2,128)(2,1)}), bf16[128,2,8192]{2,1,0:T(2,128)(2,1)}, u32[]{:S(2)}, u32[]{:S(2)}) async-start(bf16[128,2,8192]{2,1,0:T(2,128)(2,1)} %all_to_all.22), calls=%async_computation | async-start | bytes 8388608 | tf_op jit(solution)/shard_map/all_to_all | solution.py:99
  66.9 43.1 %all-to-all-done = bf16[128,2,8192]{2,1,0:T(2,128)(2,1)} async-done(((bf16[128,2,8192]{2,1,0:T(2,128)(2,1)}), bf16[128,2,8192]{2,1,0:T(2,128)(2,1)}, u32[]{:S(2)}, u32[]{:S(2)}) %all-to-all-start) | async-done | bytes 4194336 | tf_op jit(solution)/shard_map/all_to_all | solution.py:99
  110.0 7.8 %reshape.153 = bf16[2048,1024]{1,0:T(8,128)(2,1)} reshape(bf16[128,2,8192]{2,1,0:T(2,128)(2,1)} %all-to-all-done) | data formatting | bytes 8388608 | tf_op jit(solution)/shard_map/reshape | solution.py:140
  128.0 296.1 %while.18 = (s32[]{:T(128)}, bf16[8,1024,64]{1,2,0:T(8,128)(2,1)}, bf16[8,1024,64]{1,2,0:T(8,128)(2,1)}, bf16[8,2048,64]{1,2,0:T(8,128)(2,1)}, bf16[8,2048,64]{1...) while((s32[]{:T(128)}, bf16[8,1024,64]{1,2,0:T(8,128)(2,1)}, ...), condition=%wide.wide.region_7.8_spmd.clone, body=%wide.wide.region_3.7_spmd.clone.sunk | while | flops 1665336320 | bytes 125421728 | solution.py:72
  134.1 8.7 %multiply_reduce_fusion.3 = (f32[1024]{0:T(1024)S(1)}, f32[1024,2048]{1,0:T(8,128)}, f32[1024,2048]{1,0:T(8,128)}) fusion(f32[1024]{0:T(1024)S(1)} %exponential_add_fusion.3, f32[1024]{0:T(1024)S(1)} %broadcast_maximum_fusion.3, f32[2048]{0:T(1024)S(1)} %get-tuple-element.381, f32[1024,2048]{1,0:T(8,128)S(1)} %get-tuple-element.336, ...), kind=kOutput, calls=%fused_computation.8.clone.clone.1 | convolution fusion | flops 287308800 | bytes 25723904 | tf_op jit(solution)/shard_map/while/body/eval_jaxpr/dot_general | solution.py:64
  142.7 8.5 %multiply_convert_fusion.4 = bf16[1024,2048]{1,0:T(8,128)(2,1)} fusion(f32[1024,2048]{1,0:T(8,128)} %get-tuple-element.338, f32[1024,2048]{1,0:T(8,128)} %get-tuple-element.339, f32[1024]{0:T(1024)S(1)} %get-tuple-element.340), kind=kLoop, calls=%fused_computation.7.clone.clone.1 | loop fusion | flops 6291456 | bytes 20975616 | tf_op jit(solution)/shard_map/while/body/eval_jaxpr/convert_element_type | solution.py:66
  171.1 8.7 %multiply_reduce_fusion.3 = (f32[1024]{0:T(1024)S(1)}, f32[1024,2048]{1,0:T(8,128)}, f32[1024,2048]{1,0:T(8,128)}) fusion(f32[1024]{0:T(1024)S(1)} %exponential_add_fusion.3, f32[1024]{0:T(1024)S(1)} %broadcast_maximum_fusion.3, f32[2048]{0:T(1024)S(1)} %get-tuple-element.381, f32[1024,2048]{1,0:T(8,128)S(1)} %get-tuple-element.336, ...), kind=kOutput, calls=%fused_computation.8.clone.clone.1 | convolution fusion | flops 287308800 | bytes 25723904 | tf_op jit(solution)/shard_map/while/body/eval_jaxpr/dot_general | solution.py:64
  179.8 8.5 %multiply_convert_fusion.4 = bf16[1024,2048]{1,0:T(8,128)(2,1)} fusion(f32[1024,2048]{1,0:T(8,128)} %get-tuple-element.338, f32[1024,2048]{1,0:T(8,128)} %get-tuple-element.339, f32[1024]{0:T(1024)S(1)} %get-tuple-element.340), kind=kLoop, calls=%fused_computation.7.clone.clone.1 | loop fusion | flops 6291456 | bytes 20975616 | tf_op jit(solution)/shard_map/while/body/eval_jaxpr/convert_element_type | solution.py:66
  208.1 8.7 %multiply_reduce_fusion.3 = (f32[1024]{0:T(1024)S(1)}, f32[1024,2048]{1,0:T(8,128)}, f32[1024,2048]{1,0:T(8,128)}) fusion(f32[1024]{0:T(1024)S(1)} %exponential_add_fusion.3, f32[1024]{0:T(1024)S(1)} %broadcast_maximum_fusion.3, f32[2048]{0:T(1024)S(1)} %get-tuple-element.381, f32[1024,2048]{1,0:T(8,128)S(1)} %get-tuple-element.336, ...), kind=kOutput, calls=%fused_computation.8.clone.clone.1 | convolution fusion | flops 287308800 | bytes 25723904 | tf_op jit(solution)/shard_map/while/body/eval_jaxpr/dot_general | solution.py:64
  216.8 8.5 %multiply_convert_fusion.4 = bf16[1024,2048]{1,0:T(8,128)(2,1)} fusion(f32[1024,2048]{1,0:T(8,128)} %get-tuple-element.338, f32[1024,2048]{1,0:T(8,128)} %get-tuple-element.339, f32[1024]{0:T(1024)S(1)} %get-tuple-element.340), kind=kLoop, calls=%fused_computation.7.clone.clone.1 | loop fusion | flops 6291456 | bytes 20975616 | tf_op jit(solution)/shard_map/while/body/eval_jaxpr/convert_element_type | solution.py:66
  245.2 8.7 %multiply_reduce_fusion.3 = (f32[1024]{0:T(1024)S(1)}, f32[1024,2048]{1,0:T(8,128)}, f32[1024,2048]{1,0:T(8,128)}) fusion(f32[1024]{0:T(1024)S(1)} %exponential_add_fusion.3, f32[1024]{0:T(1024)S(1)} %broadcast_maximum_fusion.3, f32[2048]{0:T(1024)S(1)} %get-tuple-element.381, f32[1024,2048]{1,0:T(8,128)S(1)} %get-tuple-element.336, ...), kind=kOutput, calls=%fused_computation.8.clone.clone.1 | convolution fusion | flops 287308800 | bytes 25723904 | tf_op jit(solution)/shard_map/while/body/eval_jaxpr/dot_general | solution.py:64
  253.8 8.5 %multiply_convert_fusion.4 = bf16[1024,2048]{1,0:T(8,128)(2,1)} fusion(f32[1024,2048]{1,0:T(8,128)} %get-tuple-element.338, f32[1024,2048]{1,0:T(8,128)} %get-tuple-element.339, f32[1024]{0:T(1024)S(1)} %get-tuple-element.340), kind=kLoop, calls=%fused_computation.7.clone.clone.1 | loop fusion | flops 6291456 | bytes 20975616 | tf_op jit(solution)/shard_map/while/body/eval_jaxpr/convert_element_type | solution.py:66
  282.2 8.7 %multiply_reduce_fusion.3 = (f32[1024]{0:T(1024)S(1)}, f32[1024,2048]{1,0:T(8,128)}, f32[1024,2048]{1,0:T(8,128)}) fusion(f32[1024]{0:T(1024)S(1)} %exponential_add_fusion.3, f32[1024]{0:T(1024)S(1)} %broadcast_maximum_fusion.3, f32[2048]{0:T(1024)S(1)} %get-tuple-element.381, f32[1024,2048]{1,0:T(8,128)S(1)} %get-tuple-element.336, ...), kind=kOutput, calls=%fused_computation.8.clone.clone.1 | convolution fusion | flops 287308800 | bytes 25723904 | tf_op jit(solution)/shard_map/while/body/eval_jaxpr/dot_general | solution.py:64
  290.8 8.5 %multiply_convert_fusion.4 = bf16[1024,2048]{1,0:T(8,128)(2,1)} fusion(f32[1024,2048]{1,0:T(8,128)} %get-tuple-element.338, f32[1024,2048]{1,0:T(8,128)} %get-tuple-element.339, f32[1024]{0:T(1024)S(1)} %get-tuple-element.340), kind=kLoop, calls=%fused_computation.7.clone.clone.1 | loop fusion | flops 6291456 | bytes 20975616 | tf_op jit(solution)/shard_map/while/body/eval_jaxpr/convert_element_type | solution.py:66
  319.2 8.7 %multiply_reduce_fusion.3 = (f32[1024]{0:T(1024)S(1)}, f32[1024,2048]{1,0:T(8,128)}, f32[1024,2048]{1,0:T(8,128)}) fusion(f32[1024]{0:T(1024)S(1)} %exponential_add_fusion.3, f32[1024]{0:T(1024)S(1)} %broadcast_maximum_fusion.3, f32[2048]{0:T(1024)S(1)} %get-tuple-element.381, f32[1024,2048]{1,0:T(8,128)S(1)} %get-tuple-element.336, ...), kind=kOutput, calls=%fused_computation.8.clone.clone.1 | convolution fusion | flops 287308800 | bytes 25723904 | tf_op jit(solution)/shard_map/while/body/eval_jaxpr/dot_general | solution.py:64
  327.8 8.5 %multiply_convert_fusion.4 = bf16[1024,2048]{1,0:T(8,128)(2,1)} fusion(f32[1024,2048]{1,0:T(8,128)} %get-tuple-element.338, f32[1024,2048]{1,0:T(8,128)} %get-tuple-element.339, f32[1024]{0:T(1024)S(1)} %get-tuple-element.340), kind=kLoop, calls=%fused_computation.7.clone.clone.1 | loop fusion | flops 6291456 | bytes 20975616 | tf_op jit(solution)/shard_map/while/body/eval_jaxpr/convert_element_type | solution.py:66
  356.2 8.7 %multiply_reduce_fusion.3 = (f32[1024]{0:T(1024)S(1)}, f32[1024,2048]{1,0:T(8,128)}, f32[1024,2048]{1,0:T(8,128)}) fusion(f32[1024]{0:T(1024)S(1)} %exponential_add_fusion.3, f32[1024]{0:T(1024)S(1)} %broadcast_maximum_fusion.3, f32[2048]{0:T(1024)S(1)} %get-tuple-element.381, f32[1024,2048]{1,0:T(8,128)S(1)} %get-tuple-element.336, ...), kind=kOutput, calls=%fused_computation.8.clone.clone.1 | convolution fusion | flops 287308800 | bytes 25723904 | tf_op jit(solution)/shard_map/while/body/eval_jaxpr/dot_general | solution.py:64
  364.8 8.5 %multiply_convert_fusion.4 = bf16[1024,2048]{1,0:T(8,128)(2,1)} fusion(f32[1024,2048]{1,0:T(8,128)} %get-tuple-element.338, f32[1024,2048]{1,0:T(8,128)} %get-tuple-element.339, f32[1024]{0:T(1024)S(1)} %get-tuple-element.340), kind=kLoop, calls=%fused_computation.7.clone.clone.1 | loop fusion | flops 6291456 | bytes 20975616 | tf_op jit(solution)/shard_map/while/body/eval_jaxpr/convert_element_type | solution.py:66
  393.2 8.7 %multiply_reduce_fusion.3 = (f32[1024]{0:T(1024)S(1)}, f32[1024,2048]{1,0:T(8,128)}, f32[1024,2048]{1,0:T(8,128)}) fusion(f32[1024]{0:T(1024)S(1)} %exponential_add_fusion.3, f32[1024]{0:T(1024)S(1)} %broadcast_maximum_fusion.3, f32[2048]{0:T(1024)S(1)} %get-tuple-element.381, f32[1024,2048]{1,0:T(8,128)S(1)} %get-tuple-element.336, ...), kind=kOutput, calls=%fused_computation.8.clone.clone.1 | convolution fusion | flops 287308800 | bytes 25723904 | tf_op jit(solution)/shard_map/while/body/eval_jaxpr/dot_general | solution.py:64
  401.9 8.5 %multiply_convert_fusion.4 = bf16[1024,2048]{1,0:T(8,128)(2,1)} fusion(f32[1024,2048]{1,0:T(8,128)} %get-tuple-element.338, f32[1024,2048]{1,0:T(8,128)} %get-tuple-element.339, f32[1024]{0:T(1024)S(1)} %get-tuple-element.340), kind=kLoop, calls=%fused_computation.7.clone.clone.1 | loop fusion | flops 6291456 | bytes 20975616 | tf_op jit(solution)/shard_map/while/body/eval_jaxpr/convert_element_type | solution.py:66
  435.1 7.9 %convert_element_type.140 = bf16[128,2,8192]{2,1,0:T(2,128)(2,1)} reshape(bf16[2048,1024]{1,0:T(8,128)(2,1)} %pad_maximum_fusion) | data formatting | bytes 8388608 | tf_op jit(solution)/shard_map/convert_element_type | solution.py:93
  442.9 5.6 all-to-all-start.3
  455.0 5.1 fusion.71
  460.1 5.1 reshape.163
  471.1 28.6 %all-to-all-done.3 = bf16[128,2,8192]{2,1,0:T(2,128)(2,1)} async-done(((bf16[128,2,8192]{2,1,0:T(2,128)(2,1)}), bf16[128,2,8192]{2,1,0:T(2,128)(2,1)}, u32[]{:S(2)}, u32[]{:S(2)}) %all-to-all-start.3) | async-done | bytes 4194336 | tf_op jit(solution)/shard_map/all_to_all | solution.py:106
  499.8 7.8 %reshape.161 = bf16[2048,1024]{1,0:T(8,128)(2,1)} reshape(bf16[128,2,8192]{2,1,0:T(2,128)(2,1)} %all-to-all-done.3) | data formatting | bytes 8388608 | tf_op jit(solution)/shard_map/reshape | solution.py:156
  507.6 5.9 fusion.72
  513.5 8.7 %fusion.52 = f32[256,512]{1,0:T(8,128)} fusion(bf16[2048,256]{1,0:T(8,128)(2,1)} %reshape.158, f32[2048,512]{1,0:T(8,128)} %reshape.163, bf16[2048,1024]{1,0:T(8,128)(2,1)} %reshape.161, bf16[512,1024]{1,0:T(8,128)(2,1)S(1)} %copy-done), kind=kOutput, calls=%fused_computation.71 | convolution fusion | flops 2694840320 | bytes 11010048 | tf_op jit(solution)/shard_map/dot_general | solution.py:42
  529.6 145.8 %all-reduce.3.cloned.1.call-done = (f32[256,512]{1,0:T(8,128)}, f32[512,1024]{1,0:T(8,128)}, f32[512,512]{0,1:T(8,128)}, f32[512,512]{1,0:T(8,128)}) async-done(((f32[256,512]{1,0:T(8,128)}, f32[512,1024]{1,0:T(8,128)}, f32[512,512]{0,1:T(8,128)}, f32[512,512]{1,0:T(8,128)}), (f32[256,512]{1,0:T(8,128)}, f32[512,1024]{1,0:T(8,128)}, f32[512,512]{0,1:T(8,128)}, ...) | async-done | bytes 4718608 | tf_op jit(solution)/shard_map/psum | solution.py:158
  (169 shorter events, 231.0 us)
Async XLA Ops:
  7.2 19.1 %copy-start = (bf16[512,1024]{1,0:T(8,128)(2,1)S(1)}, bf16[512,1024]{1,0:T(8,128)(2,1)}, u32[]{:S(2)}) copy-start(bf16[512,1024]{1,0:T(8,128)(2,1)} %param.19) | copy-start | bytes 3145732
  9.5 31.4 %copy-start.9 = (bf16[256,32]{0,1:T(8,128)(2,1)}, bf16[256,32]{0,1:T(8,128)(2,1)S(1)}, u32[]{:S(2)}) copy-start(bf16[256,32]{0,1:T(8,128)(2,1)S(1)} %get-tuple-element.193) | copy-start | bytes 49156
  11.0 21.2 %all-to-all-start.1 = ((bf16[128,2,8]{2,1,0:T(2,128)(2,1)}), bf16[128,2,8]{2,1,0:T(2,128)(2,1)S(1)}, u32[]{:S(2)}, u32[]{:S(2)}) async-start(bf16[128,2,8]{2,1,0:T(2,128)(2,1)} %bitcast.5), calls=%async_computation.1 | async-start | bytes 131072 | tf_op jit(solution)/shard_map/all_to_all | solution.py:101
  25.5 0.7 copy-start.2
  32.2 16.3 %all-to-all-start.2 = ((bf16[128,2,8]{2,1,0:T(2,128)(2,1)}), bf16[128,2,8]{2,1,0:T(2,128)(2,1)S(1)}, u32[]{:S(2)}, u32[]{:S(2)}) async-start(bf16[128,2,8]{2,1,0:T(2,128)(2,1)} %bitcast.12), calls=%async_computation.2 | async-start | bytes 131072 | tf_op jit(solution)/shard_map/all_to_all | solution.py:100
  48.6 61.4 %all-to-all-start = ((bf16[128,2,8192]{2,1,0:T(2,128)(2,1)}), bf16[128,2,8192]{2,1,0:T(2,128)(2,1)}, u32[]{:S(2)}, u32[]{:S(2)}) async-start(bf16[128,2,8192]{2,1,0:T(2,128)(2,1)} %all_to_all.22), calls=%async_computation | async-start | bytes 8388608 | tf_op jit(solution)/shard_map/all_to_all | solution.py:99
  58.8 4.0 copy-start.12
  66.5 43.5 %copy-start.8 = (f32[256,8]{1,0:T(8,128)}, f32[256,8]{1,0:T(8,128)S(1)}, u32[]{:S(2)}) copy-start(f32[256,8]{1,0:T(8,128)S(1)} %convert.13) | copy-start | bytes 24580
  151.3 8.2 %copy-start.1 = (f32[1024,2048]{1,0:T(8,128)S(1)}, f32[1024,2048]{1,0:T(8,128)}, u32[]{:S(2)}) copy-start(f32[1024,2048]{1,0:T(8,128)} %get-tuple-element.338) | copy-start | bytes 25165828 | tf_op jit(solution)/shard_map/while
  188.3 8.2 %copy-start.1 = (f32[1024,2048]{1,0:T(8,128)S(1)}, f32[1024,2048]{1,0:T(8,128)}, u32[]{:S(2)}) copy-start(f32[1024,2048]{1,0:T(8,128)} %get-tuple-element.338) | copy-start | bytes 25165828 | tf_op jit(solution)/shard_map/while
  225.3 8.2 %copy-start.1 = (f32[1024,2048]{1,0:T(8,128)S(1)}, f32[1024,2048]{1,0:T(8,128)}, u32[]{:S(2)}) copy-start(f32[1024,2048]{1,0:T(8,128)} %get-tuple-element.338) | copy-start | bytes 25165828 | tf_op jit(solution)/shard_map/while
  262.3 8.2 %copy-start.1 = (f32[1024,2048]{1,0:T(8,128)S(1)}, f32[1024,2048]{1,0:T(8,128)}, u32[]{:S(2)}) copy-start(f32[1024,2048]{1,0:T(8,128)} %get-tuple-element.338) | copy-start | bytes 25165828 | tf_op jit(solution)/shard_map/while
  299.4 8.2 %copy-start.1 = (f32[1024,2048]{1,0:T(8,128)S(1)}, f32[1024,2048]{1,0:T(8,128)}, u32[]{:S(2)}) copy-start(f32[1024,2048]{1,0:T(8,128)} %get-tuple-element.338) | copy-start | bytes 25165828 | tf_op jit(solution)/shard_map/while
  336.3 8.2 %copy-start.1 = (f32[1024,2048]{1,0:T(8,128)S(1)}, f32[1024,2048]{1,0:T(8,128)}, u32[]{:S(2)}) copy-start(f32[1024,2048]{1,0:T(8,128)} %get-tuple-element.338) | copy-start | bytes 25165828 | tf_op jit(solution)/shard_map/while
  373.3 8.2 %copy-start.1 = (f32[1024,2048]{1,0:T(8,128)S(1)}, f32[1024,2048]{1,0:T(8,128)}, u32[]{:S(2)}) copy-start(f32[1024,2048]{1,0:T(8,128)} %get-tuple-element.338) | copy-start | bytes 25165828 | tf_op jit(solution)/shard_map/while
  410.4 8.2 %copy-start.1 = (f32[1024,2048]{1,0:T(8,128)S(1)}, f32[1024,2048]{1,0:T(8,128)}, u32[]{:S(2)}) copy-start(f32[1024,2048]{1,0:T(8,128)} %get-tuple-element.338) | copy-start | bytes 25165828 | tf_op jit(solution)/shard_map/while
  442.9 5.7 copy-start.3
  442.9 5.8 copy-start.10
  442.9 56.8 %all-to-all-start.3 = ((bf16[128,2,8192]{2,1,0:T(2,128)(2,1)}), bf16[128,2,8192]{2,1,0:T(2,128)(2,1)}, u32[]{:S(2)}, u32[]{:S(2)}) async-start(bf16[128,2,8192]{2,1,0:T(2,128)(2,1)} %convert_element_type.140), calls=%async_computation.3 | async-start | bytes 8388608 | tf_op jit(solution)/shard_map/all_to_all | solution.py:106
  448.6 3.5 copy-start.7
  448.6 226.9 %all-reduce.3.cloned.1.call-start = ((), (), s32[]{:S(2)}) async-start(), calls=%async_computation.4 | async-start | bytes 9437184 | tf_op jit(solution)/shard_map/psum | solution.py:158
  449.5 5.5 copy-start.11
  460.1 5.1 copy-start.15
  460.1 8.1 %copy-start.13 = (bf16[1024,512]{1,0:T(8,128)(2,1)S(1)}, bf16[1024,512]{1,0:T(8,128)(2,1)}, u32[]{:S(2)}) copy-start(bf16[1024,512]{1,0:T(8,128)(2,1)} %param.13) | copy-start | bytes 3145732
  471.1 36.5 %copy-start.4 = (bf16[2048,512]{1,0:T(8,128)(2,1)S(1)}, bf16[2048,512]{1,0:T(8,128)(2,1)}, u32[]{:S(2)}) copy-start(bf16[2048,512]{1,0:T(8,128)(2,1)} %reshape.165) | copy-start | bytes 6291460
  522.1 1.2 copy-start.14
  522.1 4.3 copy-start.16
  675.5 4.6 copy-start.5
  678.1 3.3 copy-start.6
Sparse Core Ops, SparseCore 0:
  522.3 153.1 all-reduce.2
where the time goes:
time: 692 us; the launch traced here: 689 us
  matrix products  247 us (36%)
  waiting for transfers between devices  222 us (32%)
  other arithmetic  98.8 us (14%)
  local copies, waits for them, and re-layouts  74.1 us (11%)
  starting transfers between devices  32.8 us (5%)
  between operations  14.3 us (2%)
    psum x1, waiting for transfers between devices, body(): sums = lax.psum((grad_obs, grad_kv, grad_q, grad_o), ('lat', 'lon'))  146 us
    dot_general x8, matrix products, per_head(): dprob = jnp.dot(dh, vh.T, preferred_element_type=jnp.float32)  69.3 us
    convert_element_type x8, other arithmetic, per_head(): dscore = (weights * (dprob - delta)).astype(jnp.bfloat16)  68.1 us
    all_to_all x1, waiting for transfers between devices, send_keyval(): lax.all_to_all(payload, ('lat', 'lon'), split_axis=0, concat_axis=0, tile...  43.1 us
    dot_general x8, matrix products, per_head(): dq_h = jnp.dot(dscore, kh, preferred_element_type=jnp.float32) * scale  34.1 us
    dot_general x8, matrix products, per_head(): dk_h = jnp.dot(dscore.T, qh, preferred_element_type=jnp.float32) * scale  31.6 us
    all_to_all x1, waiting for transfers between devices, return_slots(): lax.all_to_all(grads, ('lat', 'lon'), split_axis=0, concat_axis=0, tiled=...  28.6 us
    reduce_sum x8, other arithmetic, per_head(): denom = jnp.exp(-top) + jnp.sum(expd, axis=1)  25.1 us
  transfers between devices with their start and end apart: 5, of which 4 were waited for; matrix products, arithmetic and copies ran while one was open for 6% of the time, Pallas kernels for 0%

commit v1 on v0

v1 whole, which is shorter than its diff:
```python
import functools
import math

import jax
import jax.numpy as jnp
from jax import lax
from jax.experimental import pallas as pl
from jax.experimental.pallas import tpu as pltpu
from jax.sharding import PartitionSpec as P

HEADS = 8
GROUPS = 8
DEV = 128
OBS = 8
CAP = 2
CH = 256
D = 512
CELLS = 1024
GCELLS = CELLS // GROUPS
ROWS = DEV * CAP * OBS
WIDE = CH + 128
KB = 256
MAXB = 16
F32 = jnp.float32
BF16 = jnp.bfloat16
NEG = -1e30


def dot(a, b):
    return lax.dot_general(a, b, (((1,), (0,)), ((), ())), preferred_element_type=F32)


def dot_nt(a, b):
    return lax.dot_general(a, b, (((1,), (1,)), ((), ())), preferred_element_type=F32)


def dot_tn(a, b):
    return lax.dot_general(a, b, (((0,), (0,)), ((), ())), preferred_element_type=F32)


def iota(shape, dim):
    return lax.broadcasted_iota(jnp.int32, shape, dim)


def gelu_parts(x):
    a = jnp.abs(x)
    t = 1.0 / (1.0 + (0.3275911 / math.sqrt(2.0)) * a)
    e = jnp.exp(-0.5 * x * x)
    poly = t * (
        0.5 * 0.254829592
        + t * (-0.5 * 0.284496736 + t * (0.5 * 1.421413741 + t * (-0.5 * 1.453152027 + t * (0.5 * 1.061405429))))
    )
    tail = poly * e
    cdf = jnp.where(x < 0.0, tail, 1.0 - tail)
    return x * cdf, cdf + x * e * (1.0 / math.sqrt(2.0 * math.pi))


def pack_kernel(foot_ref, obs_ref, out_ref):
    slots = DEV * CAP
    tile = iota((slots, 128), 0)
    hit = jnp.zeros((slots, 128), F32)
    for f in range(4):
        hit = hit + jnp.where(foot_ref[f : f + 1, :] == tile // CAP, 1.0, 0.0)
    upper = jnp.where(iota((128, 128), 0) < iota((128, 128), 1), 1.0, 0.0).astype(BF16)
    rank = dot(hit.astype(BF16), upper)
    sel = hit * jnp.where(rank == (tile % CAP).astype(F32), 1.0, 0.0)
    widen = jnp.where(iota((128, 256), 1) // OBS == iota((128, 256), 0), 1.0, 0.0).astype(BF16)
    blocks = dot(sel.astype(BF16), widen)
    spread = jnp.broadcast_to(blocks[:, None, :], (slots, OBS, 256)).reshape(ROWS, 256)
    keep = iota((ROWS, 256), 0) % OBS == iota((ROWS, 256), 1) % OBS
    choose = jnp.where(keep, spread, 0.0).astype(BF16)
    out_ref[...] = dot(choose, obs_ref[...]).astype(BF16)


def tile_kernel(
    recv_ref, lat_ref, dout_ref, wobs_ref, wkv_ref, wq_ref, wo_ref,
    upd_ref, dlat_ref, grads_ref,
    q_s, back_s, rows_s, slope_s, enc_s, kv_s, bias_s, attn_s, attnt_s, dq_s, meta_sm,
):
    me = lax.axis_index(("lat", "lon"))

    take = jnp.where(iota((16, 128), 0) == iota((16, 128), 1), 1.0, 0.0).astype(BF16)
    meta = dot_nt(take, recv_ref[:, CH:])
    mine = (me + 1).astype(F32)
    cell = jnp.full((1, ROWS), float(GROUPS), F32)
    for f in range(4):
        cell = jnp.where(meta[5 + f : 6 + f, :] == mine, meta[1 + f : 2 + f, :], cell)
    cell = jnp.concatenate([cell[:, i * 128 : (i + 1) * 128] for i in range(16)], axis=0)
    inside = jnp.concatenate([jnp.where(cell == float(g), 1.0, 0.0) for g in range(GROUPS)], axis=0)
    r, c = iota((128, 128), 0), iota((128, 128), 1)
    upto = jnp.where(r <= c, 1.0, 0.0).astype(BF16)
    prefix = dot(inside.astype(BF16), upto)
    total = jnp.broadcast_to(prefix[:, 127:128], (128, 128)).astype(BF16)
    same = r // 16 == c // 16
    before = dot(jnp.where(same & (c < r), 1.0, 0.0).astype(BF16), total)
    count = dot(jnp.where(same, 1.0, 0.0).astype(BF16), total)
    nblk = jnp.floor((count + (KB - 1.0)) * (1.0 / KB))
    first = dot(jnp.where((c % 16 == 0) & (c // 16 < r // 16), 1.0, 0.0).astype(BF16), nblk.astype(BF16))
    place = jnp.where(inside > 0.5, first * float(KB) + before + prefix - 1.0, -1.0)
    pos = place[0:16, :]
    for g in range(1, GROUPS):
        pos = jnp.maximum(pos, place[g * 16 : (g + 1) * 16, :])
    for g in range(GROUPS):
        meta_sm[0, g] = jnp.max(first[g * 16 : g * 16 + 8, :]).astype(jnp.int32)
        meta_sm[1, g] = jnp.max(nblk[g * 16 : g * 16 + 8, :]).astype(jnp.int32)
    blocks = meta_sm[0, GROUPS - 1] + meta_sm[1, GROUPS - 1]

    q_s[...] = (dot(lat_ref[...], wq_ref[...]).astype(BF16).astype(F32) * 0.125).astype(BF16)
    back_s[...] = dot_nt(dout_ref[...], wo_ref[...]).astype(BF16)

    lane_pos = [jnp.broadcast_to(pos[i : i + 1, :], (16, 128)) for i in range(16)]
    row_id = iota((KB, 128), 0).astype(F32).astype(BF16)

    def encode(b, carry):
        base = (b * KB).astype(F32)
        r0 = pl.multiple_of(b * KB, KB)
        cols = []
        for i in range(16):
            rel = jnp.clip(lane_pos[i] - base, -1.0, float(KB)).astype(BF16)
            rel = jnp.concatenate([rel] * (KB // 16), axis=0)
            cols.append(jnp.where(row_id == rel, jnp.ones((), BF16), jnp.zeros((), BF16)))
        got = dot(jnp.concatenate(cols, axis=1), recv_ref[...])
        rows = got[:, :CH].astype(BF16)
        bias = jnp.where(got[:, CH + 15 : CH + 16] > 0.5, got[:, CH : CH + 1], NEG)
        bias_s[pl.ds(r0, KB), :] = jnp.broadcast_to(bias, (KB, 128))
        rows_s[pl.ds(r0, KB), :] = rows
        value, slope = gelu_parts(dot(rows, wobs_ref[...]))
        enc = value.astype(BF16)
        slope_s[pl.ds(r0, KB), :] = slope
        enc_s[pl.ds(r0, KB), :] = enc
        kv_s[pl.ds(r0, KB), :] = dot(enc, wkv_ref[...]).astype(BF16)
        return carry

    lax.fori_loop(0, blocks, encode, 0)

    lane_head = iota((GCELLS, 256), 1) // 64

    def spread_heads(x):
        return jnp.concatenate([jnp.where(lane_head == h, x, jnp.zeros((), BF16)) for h in range(4)], axis=0)

    def scores(r0, half, qq):
        keys = kv_s[pl.ds(r0, KB), half * 256 : half * 256 + 256]
        bias = bias_s[pl.ds(r0, KB), :]
        return dot_nt(keys, qq) + jnp.concatenate([bias] * 4, axis=1)

    def dprobs(r0, half, bb):
        return dot_nt(kv_s[pl.ds(r0, KB), D + half * 256 : D + half * 256 + 256], bb)

    def diagonal(x):
        return jnp.concatenate([x[h * 64 : h * 64 + 64, h * 128 : h * 128 + 128] for h in range(4)], axis=0)

    def finish(r0, half, weights, dp, delta, qq, bb):
        wb = weights.astype(BF16)
        ds = (weights * (dp - delta)).astype(BF16)
        klane, vlane = half * 256, D + half * 256
        keys = kv_s[pl.ds(r0, KB), klane : klane + 256]
        values = kv_s[pl.ds(r0, KB), vlane : vlane + 256]
        attn = diagonal(dot(values.T, wb))
        dq = diagonal(dot(keys.T, ds))
        kv_s[pl.ds(r0, KB), klane : klane + 256] = dot(ds, qq).astype(BF16)
        kv_s[pl.ds(r0, KB), vlane : vlane + 256] = dot(wb, bb).astype(BF16)
        return attn, dq

    def group(g, carry):
        start, nb = meta_sm[0, g], meta_sm[1, g]
        c0 = pl.multiple_of(g * GCELLS, GCELLS)

        def put(half, attn, dq):
            lanes = slice(half * 256, half * 256 + 256)
            at = attn.astype(BF16)
            attnt_s[g, lanes, :] = at
            attn_s[pl.ds(c0, GCELLS), lanes] = at.T
            dq_s[pl.ds(c0, GCELLS), lanes] = (dq * 0.125).astype(BF16).T

        def heads(half):
            lanes = slice(half * 256, half * 256 + 256)
            return spread_heads(q_s[pl.ds(c0, GCELLS), lanes]), spread_heads(back_s[pl.ds(c0, GCELLS), lanes])

        @pl.when(nb == 1)
        def _():
            r0 = pl.multiple_of(start * KB, KB)
            for half in range(2):
                qq, bb = heads(half)
                s = scores(r0, half, qq)
                top = jnp.maximum(jnp.max(s, axis=0, keepdims=True), 0.0)
                p = jnp.exp(s - top)
                inv = 1.0 / (jnp.exp(-top) + jnp.sum(p, axis=0, keepdims=True))
                weights = p * inv
                dp = dprobs(r0, half, bb)
                delta = jnp.sum(weights * dp, axis=0, keepdims=True)
                put(half, *finish(r0, half, weights, dp, delta, qq, bb))

        @pl.when(nb != 1)
        def _():
            for half in range(2):
                qq, bb = heads(half)

                def row(b):
                    return pl.multiple_of((start + b) * KB, KB)

                def first_pass(b, top):
                    return jnp.maximum(top, jnp.max(scores(row(b), half, qq), axis=0, keepdims=True))

                top = lax.fori_loop(0, nb, first_pass, jnp.zeros((1, 512), F32))

                def second_pass(b, sums):
                    p = jnp.exp(scores(row(b), half, qq) - top)
                    dp = dprobs(row(b), half, bb)
                    return (
                        sums[0] + jnp.sum(p, axis=0, keepdims=True),
                        sums[1] + jnp.sum(p * dp, axis=0, keepdims=True),
                    )

                sums = lax.fori_loop(0, nb, second_pass, (jnp.exp(-top), jnp.zeros((1, 512), F32)))
                inv = 1.0 / sums[0]
                delta = sums[1] * inv

                def third_pass(b, acc):
                    weights = jnp.exp(scores(row(b), half, qq) - top) * inv
                    dp = dprobs(row(b), half, bb)
                    attn, dq = finish(row(b), half, weights, dp, delta, qq, bb)
                    return acc[0] + attn, acc[1] + dq

                zero = jnp.zeros((256, GCELLS), F32)
                put(half, *lax.fori_loop(0, nb, third_pass, (zero, zero)))

        return carry

    lax.fori_loop(0, GROUPS, group, 0)

    attn, dq = attn_s[...], dq_s[...]
    upd_ref[...] = (lat_ref[...].astype(F32) + dot(attn, wo_ref[...])).astype(BF16)
    dlat_ref[...] = (dout_ref[...].astype(F32) + dot_nt(dq, wq_ref[...])).astype(BF16)
    grads_ref[1280:1792, :] = dot_tn(lat_ref[...], dq)
    attnt = jnp.concatenate([attnt_s[g] for g in range(GROUPS)], axis=1)
    grads_ref[1792:2304, :] = dot(attnt, dout_ref[...])

    grads_ref[0:1280, :] = jnp.zeros((1280, D), F32)

    def encoder_grads(b, carry):
        r0 = pl.multiple_of(b * KB, KB)
        dkv = kv_s[pl.ds(r0, KB), :]
        denc = dot_nt(dkv, wkv_ref[...])
        dpre = (denc * slope_s[pl.ds(r0, KB), :]).astype(BF16)
        grads_ref[0:256, :] += dot_tn(rows_s[pl.ds(r0, KB), :], dpre)
        part = dot_tn(enc_s[pl.ds(r0, KB), :], dkv)
        grads_ref[256:768, :] += part[:, :D]
        grads_ref[768:1280, :] += part[:, D:]
        return carry

    lax.fori_loop(0, blocks, encoder_grads, 0)


def body(latents, d_out, observations, obs_bias, footprint, obs_cell, w_obs, w_kv, w_q, w_o):
    blocks = observations.shape[0]
    rows = blocks * OBS
    foot = jnp.pad(footprint.T, ((0, 4), (0, 128 - blocks)), constant_values=-1)
    one = jnp.ones((rows, 1), BF16)
    meta = jnp.concatenate(
        [
            obs_bias.reshape(rows, 1),
            obs_cell.transpose(0, 2, 1).reshape(rows, 4).astype(BF16),
            jnp.broadcast_to(footprint[:, None, :] + 1, (blocks, OBS, 4)).reshape(rows, 4).astype(BF16),
            jnp.zeros((rows, 6), BF16),
            one,
            jnp.zeros((rows, 112), BF16),
        ],
        axis=1,
    )
    wide = jnp.concatenate([observations.reshape(rows, CH), meta], axis=1)
    vmem = pl.BlockSpec(memory_space=pltpu.VMEM)
    payload = pl.pallas_call(
        pack_kernel,
        out_shape=jax.ShapeDtypeStruct((ROWS, WIDE), BF16),
        in_specs=[vmem] * 2,
        out_specs=vmem,
        compiler_params=pltpu.CompilerParams(vmem_limit_bytes=40 << 20),
        name="pack",
    )(foot, wide)
    recv = lax.all_to_all(payload, ("lat", "lon"), split_axis=0, concat_axis=0, tiled=True)
    upd, dlat, grads = pl.pallas_call(
        tile_kernel,
        out_shape=(
            jax.ShapeDtypeStruct((CELLS, D), BF16),
            jax.ShapeDtypeStruct((CELLS, D), BF16),
            jax.ShapeDtypeStruct((2304, D), F32),
        ),
        in_specs=[vmem] * 7,
        out_specs=(vmem, vmem, vmem),
        scratch_shapes=[
            pltpu.VMEM((CELLS, D), BF16),
            pltpu.VMEM((CELLS, D), BF16),
            pltpu.VMEM((MAXB * KB, CH), BF16),
            pltpu.VMEM((MAXB * KB, D), F32),
            pltpu.VMEM((MAXB * KB, D), BF16),
            pltpu.VMEM((MAXB * KB, 2 * D), BF16),
            pltpu.VMEM((MAXB * KB, 128), F32),
            pltpu.VMEM((CELLS, D), BF16),
            pltpu.VMEM((GROUPS, D, GCELLS), BF16),
            pltpu.VMEM((CELLS, D), BF16),
            pltpu.SMEM((2, GROUPS), jnp.int32),
        ],
        compiler_params=pltpu.CompilerParams(vmem_limit_bytes=60 << 20),
        name="tile",
    )(recv, latents, d_out, w_obs, w_kv, w_q, w_o)
    grads = lax.psum(grads, ("lat", "lon"))
    gkv = jnp.concatenate([grads[256:768], grads[768:1280]], axis=1)
    return upd, dlat, grads[0:256], gkv, grads[1280:1792], grads[1792:2304]


def solution(mesh):
    spread = ("lat", "lon")
    placed = (
        P(spread, None), P(spread, None), P(spread, None, None), P(spread, None), P(spread, None),
        P(spread, None, None), P(), P(), P(), P(),
    )
    return jax.shard_map(
        body,
        mesh=mesh,
        in_specs=placed,
        out_specs=(P(spread, None), P(spread, None), P(), P(), P(), P()),
        check_vma=False,
    )
```

time: 692 us -> 263 us (0.38)
  matrix products: 247 us -> 0 us
  other arithmetic: 98.8 us -> 2.92 us
  local copies, waits for them, and re-layouts: 74.1 us -> 8.94 us
  waiting for transfers between devices: 222 us -> 158 us
  Pallas kernels: 0 us -> 43.7 us
  blocking collectives: 0 us -> 35.5 us
  starting transfers between devices: 32.8 us -> 0.04 us
    dot_general x65 -> x0, matrix products: 247 us -> none  [the longest x8 69.3 us: per_head(): dprob = jnp.dot(dh, vh.T, preferred_element_type=jnp.float32)]
    all_to_all x4 -> x0, waiting for transfers between devices: 76.1 us -> none  [the longest x1 43.1 us: send_keyval(): lax.all_to_all(payload, ('lat', 'lon'), split_axis=0, concat_axis=0, tile...]
    convert_element_type x12 -> x2, other arithmetic: 69 us -> 1.41 us  [the longest x1 0.72 us: body(): obs_cell.transpose(0, 2, 1).reshape(rows, 4).astype(BF16)]
    pallas_call x0 -> x2, Pallas kernels: none -> 43.7 us  [the longest x1 42.8 us: body(): pl.pallas_call(tile_kernel, out_shape=(jax.ShapeDtypeStruct((CELLS, D), B...]
    reshape x13 -> x1, local copies, waits for them, and re-layouts: 36.8 us -> 0.09 us  [body(): obs_bias.reshape(rows, 1)]
    all_to_all x0 -> x1, blocking collectives: none -> 35.5 us  [body(): lax.all_to_all(payload, ('lat', 'lon'), split_axis=0, concat_axis=0, tile...]
    all_to_all x4 -> x0, starting transfers between devices: 32.8 us -> none  [the longest x1 11.5 us: send_keyval(): lax.all_to_all(bias_sent, ('lat', 'lon'), split_axis=0, concat_axis=0, ti...]
    reduce_sum x10 -> x0, other arithmetic: 25.4 us -> none  [the longest x8 25.1 us: per_head(): denom = jnp.exp(-top) + jnp.sum(expd, axis=1)]
  transfers between devices with their start and end apart: 5 -> 1, of which waited for: 4 -> 1; matrix products, arithmetic and copies ran while one was open for 6% -> 0% of each run, Pallas kernels for 0% -> 0%
where the time goes in v1:
time: 263 us
  waiting for transfers between devices  158 us (60%)
  Pallas kernels  43.7 us (17%)
  blocking collectives  35.5 us (13%)
  between operations  14.1 us (5%)
  local copies, waits for them, and re-layouts  8.94 us (3%)
  other arithmetic  2.92 us (1%)
    psum x1, waiting for transfers between devices, body(): grads = lax.psum(grads, ('lat', 'lon'))  158 us
    pallas_call x1, Pallas kernels, body(): pl.pallas_call(tile_kernel, out_shape=(jax.ShapeDtypeStruct((CELLS, D), B...  42.8 us
    all_to_all x1, blocking collectives, body(): lax.all_to_all(payload, ('lat', 'lon'), split_axis=0, concat_axis=0, tile...  35.5 us
    slice x2, local copies, waits for them, and re-layouts, body(): return (upd, dlat, grads[0:256], gkv, grads[1280:1792], grads[1792:2304])  6 us
  transfers between devices with their start and end apart: 1, of which 1 were waited for; matrix products, arithmetic and copies ran while one was open for 0% of the time, Pallas kernels for 0%

profile of v1, /device:TPU:1, one launch (start us, length us, event | category | flops | bytes accessed | tf_op | source)
XLA Modules:
  0.0 263.0 jit_solution(8594520172338463983)
XLA Ops:
  7.2 0.0 all-reduce.3.cloned.1.call-start
  7.2 0.7 add_convert_fusion
  7.9 0.1 copy.21
  8.0 0.8 copy.19
  8.8 0.7 convert_bitcast_fusion
  9.5 0.2 copy.20
  9.7 0.1 reshape.28
  9.8 0.7 pad.4.foot_ref
  10.5 1.1 concatenate.6.obs_ref
  11.6 1.0 pack.1
  12.6 35.5 %all_to_all.11 = bf16[128,16,384]{2,1,0:T(8,128)(2,1)} all-to-all(bf16[128,16,384]{2,1,0:T(8,128)(2,1)S(1)} %bitcast.9), channel_id=1, replica_groups=mesh['lat'=8,'lon'=16] {'lat','lon'}, dimensions={0} | all-to-all | bytes 3145728 | tf_op jit(solution)/shard_map/all_to_all | solution.py:280
  48.1 42.8 %tile.1 = (bf16[1024,512]{1,0:T(8,128)(2,1)}, bf16[1024,512]{1,0:T(8,128)(2,1)}, f32[2304,512]{1,0:T(8,128)}) custom-call(bf16[2048,384]{1,0:T(8,128)(2,1)} %bitcast.10, bf16[1024,512]{1,0:T(8,128)(2,1)} %lat_ref.1, bf16[1024,512]{1,0:T(8,128)(2,1)} %dout_ref.1, bf16[256,512]{1,0:T(8,128)(2,1)} %wobs_ref.1, bf16[512,1024]{1,0:T(8,128)(2,1)} %wkv_ref.1, ...), custom_call_target="tpu_custom_call" | custom-call | tf_op jit(solution)/shard_map/tile/pallas_call | solution.py:281
  90.9 0.0 all-reduce.3.cloned.1.call-update
  90.9 157.7 %all-reduce.3.cloned.1.call-done = f32[2304,512]{1,0:T(8,128)} async-done(((f32[2304,512]{1,0:T(8,128)}), f32[2304,512]{1,0:T(8,128)}) %all-reduce.3.cloned.1.call-update) | async-done | bytes 4718608 | tf_op jit(solution)/shard_map/psum | solution.py:306
  248.6 4.1 %fusion = (f32[512,512]{1,0:T(8,128)}, f32[512,512]{1,0:T(8,128)}, f32[512,512]{1,0:T(8,128)S(1)}, f32[512,512]{1,0:T(8,128)S(1)}) fusion(f32[2304,512]{1,0:T(8,128)} %all-reduce.3.cloned.1.call-done), kind=kLoop, calls=%fused_computation.4 | loop fusion | bytes 8388608 | tf_op jit(solution)/shard_map/slice | solution.py:308
  252.8 1.5 pad_maximum_fusion
  254.3 1.9 slice.20
  (4 shorter events, 0.0 us)
Async XLA Ops:
  7.2 241.5 %all-reduce.3.cloned.1.call-start = ((), (), s32[]{:S(2)}) async-start(), calls=%async_computation.1 | async-start | bytes 9437184 | tf_op jit(solution)/shard_map/psum | solution.py:306
Sparse Core Ops, SparseCore 0:
  91.0 157.5 all-reduce.2

commit v2 on v1

--- a/solution.py
+++ b/solution.py
@@ -24,6 +24,7 @@
 F32 = jnp.float32
 BF16 = jnp.bfloat16
 NEG = -1e30
+MESH = pl.DeviceIdType.MESH
 
 
 def dot(a, b):
@@ -75,7 +76,7 @@
 def tile_kernel(
     recv_ref, lat_ref, dout_ref, wobs_ref, wkv_ref, wq_ref, wo_ref,
     upd_ref, dlat_ref, grads_ref,
-    q_s, back_s, rows_s, slope_s, enc_s, kv_s, bias_s, attn_s, attnt_s, dq_s, meta_sm,
+    q_s, back_s, rows_s, slope_s, enc_s, kv_s, bias_s, attn_s, attnt_s, dq_s, sums_s, meta_sm,
 ):
     me = lax.axis_index(("lat", "lon"))
 
@@ -231,24 +232,192 @@
     attn, dq = attn_s[...], dq_s[...]
     upd_ref[...] = (lat_ref[...].astype(F32) + dot(attn, wo_ref[...])).astype(BF16)
     dlat_ref[...] = (dout_ref[...].astype(F32) + dot_nt(dq, wq_ref[...])).astype(BF16)
-    grads_ref[1280:1792, :] = dot_tn(lat_ref[...], dq)
+    grads_ref[1280:1792, :] = dot_tn(lat_ref[...], dq).astype(BF16)
     attnt = jnp.concatenate([attnt_s[g] for g in range(GROUPS)], axis=1)
-    grads_ref[1792:2304, :] = dot(attnt, dout_ref[...])
-
-    grads_ref[0:1280, :] = jnp.zeros((1280, D), F32)
+    grads_ref[1792:2304, :] = dot(attnt, dout_ref[...]).astype(BF16)
+
+    sums_s[...] = jnp.zeros((1280, D), F32)
 
     def encoder_grads(b, carry):
         r0 = pl.multiple_of(b * KB, KB)
         dkv = kv_s[pl.ds(r0, KB), :]
         denc = dot_nt(dkv, wkv_ref[...])
         dpre = (denc * slope_s[pl.ds(r0, KB), :]).astype(BF16)
-        grads_ref[0:256, :] += dot_tn(rows_s[pl.ds(r0, KB), :], dpre)
+        sums_s[0:256, :] += dot_tn(rows_s[pl.ds(r0, KB), :], dpre)
         part = dot_tn(enc_s[pl.ds(r0, KB), :], dkv)
-        grads_ref[256:768, :] += part[:, :D]
-        grads_ref[768:1280, :] += part[:, D:]
+        sums_s[256:768, :] += part[:, :D]
+        sums_s[768:1280, :] += part[:, D:]
         return carry
 
     lax.fori_loop(0, blocks, encoder_grads, 0)
+    grads_ref[0:1280, :] = sums_s[...].astype(BF16)
+
+
+PARTS = 3
+HALF = 1152
+PROWS = 384
+PIECE = 96
+
+
+def peer(step_axis, k):
+    lat, lon = lax.axis_index("lat"), lax.axis_index("lon")
+    y, core, z, x = lat // 2, lat % 2, lon // 4, lon % 4
+    if step_axis == "x":
+        x = (x + k) % 4
+    elif step_axis == "y":
+        y = (y + k) % 4
+    elif step_axis == "z":
+        z = (z + k) % 4
+    else:
+        core = 1 - core
+    return {"lat": y * 2 + core, "lon": z * 4 + x}
+
+
+def place_on(step_axis):
+    lat, lon = lax.axis_index("lat"), lax.axis_index("lon")
+    return {"x": lon % 4, "y": lat // 2, "z": lon // 4}[step_axis]
+
+
+def sum_kernel(
+    g_ref, out_ref,
+    core_recv, src1, recv1, src2, recv2, buf3, full, other,
+    sem_core, sem1, sem2, sem3, sem4, sem5, sem6,
+):
+    core = lax.axis_index("lat") % 2
+    order = ("x", "y", "z")
+    barrier = pltpu.get_barrier_semaphore()
+    pl.semaphore_signal(barrier, inc=1, device_id=peer("core", 1), device_id_type=MESH)
+    for axis in order:
+        for k in range(1, 4):
+            pl.semaphore_signal(barrier, inc=1, device_id=peer(axis, k), device_id_type=MESH)
+    pl.semaphore_wait(barrier, 10)
+
+    def send(src, dst, sems, axis, k):
+        copy = pltpu.make_async_remote_copy(
+            src_ref=src, dst_ref=dst, send_sem=sems.at[0], recv_sem=sems.at[1],
+            device_id=peer(axis, k), device_id_type=MESH,
+        )
+        copy.start()
+        return copy
+
+    mine = pl.multiple_of(core * HALF, HALF)
+    theirs = pl.multiple_of((1 - core) * HALF, HALF)
+    copies = []
+    first = []
+    for p in range(PARTS):
+        first.append(
+            send(g_ref.at[pl.ds(theirs + p * PROWS, PROWS), :], core_recv.at[p], sem_core.at[p], "core", 1)
+        )
+    second = []
+    for p in range(PARTS):
+        axis = order[p]
+        first[p].wait_recv()
+        for j in range(4):
+            own = g_ref[pl.ds(mine + p * PROWS + j * PIECE, PIECE), :].astype(F32)
+            src1[p, j] = (own + core_recv[p, j * PIECE : (j + 1) * PIECE, :].astype(F32)).astype(BF16)
+        at = place_on(axis)
+        second.append([
+            send(src1.at[p, (at + k) % 4], recv1.at[p, k - 1], sem1.at[p, k - 1], axis, k) for k in range(1, 4)
+        ])
+    third = []
+    for p in range(PARTS):
+        axis, nxt = order[p], order[(p + 1) % 3]
+        for copy in second[p]:
+            copy.wait_recv()
+        total = src1[p, place_on(axis)].astype(F32)
+        for k in range(3):
+            total = total + recv1[p, k].astype(F32)
+        for j in range(4):
+            src2[p, j] = total[:, j * 128 : (j + 1) * 128].astype(BF16)
+        at = place_on(nxt)
+        third.append([
+            send(src2.at[p, (at + k) % 4], recv2.at[p, k - 1], sem2.at[p, k - 1], nxt, k) for k in range(1, 4)
+        ])
+    fourth = []
+    for p in range(PARTS):
+        axis, nxt = order[(p + 1) % 3], order[(p + 2) % 3]
+        for copy in third[p]:
+            copy.wait_recv()
+        total = src2[p, place_on(axis)].astype(F32)
+        for k in range(3):
+            total = total + recv2[p, k].astype(F32)
+        buf3[p, 0] = total.astype(BF16)
+        fourth.append([send(buf3.at[p, 0], buf3.at[p, k], sem3.at[p, k - 1], nxt, k) for k in range(1, 4)])
+    fifth = []
+    for p in range(PARTS):
+        a1, a2, a3 = order[p], order[(p + 1) % 3], order[(p + 2) % 3]
+        for copy in fourth[p]:
+            copy.wait_recv()
+        at = place_on(a3)
+        total = buf3[p, at].astype(F32)
+        for s in range(1, 4):
+            total = total + buf3[p, (at + 4 - s) % 4].astype(F32)
+        i, j = place_on(a1), place_on(a2)
+        full[p, i, j] = total.astype(BF16)
+        fifth.append([send(full.at[p, i, j], full.at[p, i, j], sem4.at[p, k - 1], a2, k) for k in range(1, 4)])
+    sixth = []
+    for p in range(PARTS):
+        a1 = order[p]
+        for copy in fifth[p]:
+            copy.wait_recv()
+        i = place_on(a1)
+        sixth.append([send(full.at[p, i], full.at[p, i], sem5.at[p, k - 1], a1, k) for k in range(1, 4)])
+    last = []
+    for p in range(PARTS):
+        for copy in sixth[p]:
+            copy.wait_recv()
+        last.append(send(full.at[p], other.at[p], sem6.at[p], "core", 1))
+        for i in range(4):
+            for j in range(4):
+                out_ref[pl.ds(mine + p * PROWS + i * PIECE, PIECE), j * 128 : (j + 1) * 128] = full[p, i, j]
+    for p in range(PARTS):
+        last[p].wait_recv()
+        for i in range(4):
+            for j in range(4):
+                out_ref[pl.ds(theirs + p * PROWS + i * PIECE, PIECE), j * 128 : (j + 1) * 128] = other[p, i, j]
+    for p in range(PARTS):
+        for copy in [first[p], last[p]] + second[p] + third[p] + fourth[p] + fifth[p] + sixth[p]:
+            copy.wait_send()
+
+
+def widen_kernel(g_ref, obs_ref, kv_ref, q_ref, o_ref):
+    obs_ref[...] = g_ref[0:256, :].astype(F32)
+    kv_ref[:, :D] = g_ref[256:768, :].astype(F32)
+    kv_ref[:, D:] = g_ref[768:1280, :].astype(F32)
+    q_ref[...] = g_ref[1280:1792, :].astype(F32)
+    o_ref[...] = g_ref[1792:2304, :].astype(F32)
+
+
+def sum_grads(grads):
+    vmem = pl.BlockSpec(memory_space=pltpu.VMEM)
+    dma = pltpu.SemaphoreType.DMA
+    return pl.pallas_call(
+        sum_kernel,
+        out_shape=jax.ShapeDtypeStruct((2 * HALF, D), BF16),
+        in_specs=[vmem],
+        out_specs=vmem,
+        scratch_shapes=[
+            pltpu.VMEM((PARTS, PROWS, D), BF16),
+            pltpu.VMEM((PARTS, 4, PIECE, D), BF16),
+            pltpu.VMEM((PARTS, 3, PIECE, D), BF16),
+            pltpu.VMEM((PARTS, 4, PIECE, 128), BF16),
+            pltpu.VMEM((PARTS, 3, PIECE, 128), BF16),
+            pltpu.VMEM((PARTS, 4, PIECE, 128), BF16),
+            pltpu.VMEM((PARTS, 4, 4, PIECE, 128), BF16),
+            pltpu.VMEM((PARTS, 4, 4, PIECE, 128), BF16),
+            dma((PARTS, 2)),
+            dma((PARTS, 3, 2)),
+            dma((PARTS, 3, 2)),
+            dma((PARTS, 3, 2)),
+            dma((PARTS, 3, 2)),
+            dma((PARTS, 3, 2)),
+            dma((PARTS, 2)),
+        ],
+        compiler_params=pltpu.CompilerParams(
+            collective_id=1, has_side_effects=True, vmem_limit_bytes=40 << 20
+        ),
+        name="sum_grads",
+    )(grads)
 
 
 def body(latents, d_out, observations, obs_bias, footprint, obs_cell, w_obs, w_kv, w_q, w_o):
@@ -283,7 +452,7 @@
         out_shape=(
             jax.ShapeDtypeStruct((CELLS, D), BF16),
             jax.ShapeDtypeStruct((CELLS, D), BF16),
-            jax.ShapeDtypeStruct((2304, D), F32),
+            jax.ShapeDtypeStruct((2304, D), BF16),
         ),
         in_specs=[vmem] * 7,
         out_specs=(vmem, vmem, vmem),
@@ -298,14 +467,21 @@
             pltpu.VMEM((CELLS, D), BF16),
             pltpu.VMEM((GROUPS, D, GCELLS), BF16),
             pltpu.VMEM((CELLS, D), BF16),
+            pltpu.VMEM((1280, D), F32),
             pltpu.SMEM((2, GROUPS), jnp.int32),
         ],
         compiler_params=pltpu.CompilerParams(vmem_limit_bytes=60 << 20),
         name="tile",
     )(recv, latents, d_out, w_obs, w_kv, w_q, w_o)
-    grads = lax.psum(grads, ("lat", "lon"))
-    gkv = jnp.concatenate([grads[256:768], grads[768:1280]], axis=1)
-    return upd, dlat, grads[0:256], gkv, grads[1280:1792], grads[1792:2304]
+    gobs, gkv, gq, go = pl.pallas_call(
+        widen_kernel,
+        out_shape=[jax.ShapeDtypeStruct(x.shape, F32) for x in (w_obs, w_kv, w_q, w_o)],
+        in_specs=[vmem],
+        out_specs=[vmem] * 4,
+        compiler_params=pltpu.CompilerParams(vmem_limit_bytes=40 << 20),
+        name="widen",
+    )(sum_grads(grads))
+    return upd, dlat, gobs, gkv, gq, go
 
 
 def solution(mesh):

time: 263 us -> 119 us (0.45)
  waiting for transfers between devices: 158 us -> 0 us
  Pallas kernels: 43.7 us -> 76.9 us
  between operations: 14.1 us -> 0.68 us
  local copies, waits for them, and re-layouts: 8.94 us -> 4.61 us
    psum x1 -> x0, waiting for transfers between devices: 158 us -> none  [body(): grads = lax.psum(grads, ('lat', 'lon'))]
    pallas_call x0 -> x2, Pallas kernels: none -> 33.9 us  [the longest x1 31.6 us: sum_grads(): pl.pallas_call(sum_kernel, out_shape=jax.ShapeDtypeStruct((2 * HALF, D),...]
    slice x2 -> x0, local copies, waits for them, and re-layouts: 6 us -> none  [body(): return (upd, dlat, grads[0:256], gkv, grads[1280:1792], grads[1792:2304])]
  transfers between devices with their start and end apart: 1 -> 0, of which waited for: 1 -> 0; matrix products, arithmetic and copies ran while one was open for 0% -> 0% of each run, Pallas kernels for 0% -> 0%
where the time goes in v2:
time: 119 us
  Pallas kernels  76.9 us (65%)
  blocking collectives  35.5 us (30%)
  local copies, waits for them, and re-layouts  4.61 us (4%)
  other arithmetic  1.41 us (1%)
    pallas_call x1, Pallas kernels, body(): pl.pallas_call(tile_kernel, out_shape=(jax.ShapeDtypeStruct((CELLS, D), B...  42 us
    all_to_all x1, blocking collectives, body(): lax.all_to_all(payload, ('lat', 'lon'), split_axis=0, concat_axis=0, tile...  35.5 us
    pallas_call x1, Pallas kernels, sum_grads(): pl.pallas_call(sum_kernel, out_shape=jax.ShapeDtypeStruct((2 * HALF, D),...  31.6 us
    unnamed x3, local copies, waits for them, and re-layouts  2.43 us

profile of v2, /device:TPU:1, one launch (start us, length us, event | category | flops | bytes accessed | tf_op | source)
XLA Modules:
  0.0 119.1 jit_solution(4705404119371007725)
XLA Ops:
  0.6 0.7 add_convert_fusion
  1.3 0.1 copy.21
  1.4 0.8 copy.19
  2.2 0.7 convert_bitcast_fusion
  2.9 0.2 copy.20
  3.1 0.1 reshape.28
  3.2 0.7 pad.4.foot_ref
  3.9 1.1 concatenate.3.obs_ref
  5.0 1.0 pack.1
  6.0 35.5 %all_to_all.11 = bf16[128,16,384]{2,1,0:T(8,128)(2,1)} all-to-all(bf16[128,16,384]{2,1,0:T(8,128)(2,1)S(1)} %bitcast.9), channel_id=1, replica_groups=mesh['lat'=8,'lon'=16] {'lat','lon'}, dimensions={0} | all-to-all | bytes 3145728 | tf_op jit(solution)/shard_map/all_to_all | solution.py:449
  41.5 42.0 %tile.1 = (bf16[1024,512]{1,0:T(8,128)(2,1)}, bf16[1024,512]{1,0:T(8,128)(2,1)}, bf16[2304,512]{1,0:T(8,128)(2,1)}) custom-call(bf16[2048,384]{1,0:T(8,128)(2,1)} %bitcast.10, bf16[1024,512]{1,0:T(8,128)(2,1)} %lat_ref.1, bf16[1024,512]{1,0:T(8,128)(2,1)} %dout_ref.1, bf16[256,512]{1,0:T(8,128)(2,1)} %wobs_ref.1, bf16[512,1024]{1,0:T(8,128)(2,1)} %wkv_ref.1, ...), custom_call_target="tpu_custom_call" | custom-call | tf_op jit(solution)/shard_map/tile/pallas_call | solution.py:450
  83.6 0.0 copy-start
  83.6 1.7 %copy-done = bf16[2304,512]{1,0:T(8,128)(2,1)S(1)} copy-done((bf16[2304,512]{1,0:T(8,128)(2,1)S(1)}, bf16[2304,512]{1,0:T(8,128)(2,1)}, u32[]{:S(2)}) %copy-start) | copy-done | bytes 2359320
  85.2 31.6 %sum_grads.1.g_ref = bf16[2304,512]{1,0:T(8,128)(2,1)S(1)} custom-call(bf16[2304,512]{1,0:T(8,128)(2,1)S(1)} %copy-done), custom_call_target="tpu_custom_call" | custom-call | tf_op jit(solution)/shard_map/sum_grads/pallas_call | solution.py:394
  116.8 2.3 %widen.1 = (f32[256,512]{1,0:T(8,128)}, f32[512,1024]{1,0:T(8,128)}, f32[512,512]{1,0:T(8,128)}, f32[512,512]{1,0:T(8,128)}) custom-call(bf16[2304,512]{1,0:T(8,128)(2,1)S(1)} %sum_grads.1.g_ref), custom_call_target="tpu_custom_call" | custom-call | tf_op jit(solution)/shard_map/widen/pallas_call | solution.py:476
  (4 shorter events, 0.0 us)
Async XLA Ops:
  83.6 1.7 %copy-start = (bf16[2304,512]{1,0:T(8,128)(2,1)S(1)}, bf16[2304,512]{1,0:T(8,128)(2,1)}, u32[]{:S(2)}) copy-start(bf16[2304,512]{1,0:T(8,128)(2,1)} %get-tuple-element.15.g_ref) | copy-start | bytes 7077892

commit v3 on v1

--- a/solution.py
+++ b/solution.py
@@ -18,12 +18,14 @@
 CELLS = 1024
 GCELLS = CELLS // GROUPS
 ROWS = DEV * CAP * OBS
-WIDE = CH + 128
 KB = 256
-MAXB = 16
+MAXB = 15
+LEAD = 8
 F32 = jnp.float32
 BF16 = jnp.bfloat16
 NEG = -1e30
+VMEM_LIMIT = 59 << 20
+MESH = pl.DeviceIdType.MESH
 
 
 def dot(a, b):
@@ -55,39 +57,161 @@
     return x * cdf, cdf + x * e * (1.0 / math.sqrt(2.0 * math.pi))
 
 
-def pack_kernel(foot_ref, obs_ref, out_ref):
-    slots = DEV * CAP
-    tile = iota((slots, 128), 0)
-    hit = jnp.zeros((slots, 128), F32)
-    for f in range(4):
-        hit = hit + jnp.where(foot_ref[f : f + 1, :] == tile // CAP, 1.0, 0.0)
-    upper = jnp.where(iota((128, 128), 0) < iota((128, 128), 1), 1.0, 0.0).astype(BF16)
-    rank = dot(hit.astype(BF16), upper)
-    sel = hit * jnp.where(rank == (tile % CAP).astype(F32), 1.0, 0.0)
-    widen = jnp.where(iota((128, 256), 1) // OBS == iota((128, 256), 0), 1.0, 0.0).astype(BF16)
-    blocks = dot(sel.astype(BF16), widen)
-    spread = jnp.broadcast_to(blocks[:, None, :], (slots, OBS, 256)).reshape(ROWS, 256)
-    keep = iota((ROWS, 256), 0) % OBS == iota((ROWS, 256), 1) % OBS
-    choose = jnp.where(keep, spread, 0.0).astype(BF16)
-    out_ref[...] = dot(choose, obs_ref[...]).astype(BF16)
+def hot(mask):
+    return jnp.where(mask, 1.0, 0.0).astype(BF16)
+
+
+def exchange_kernel(
+    foot_ref, obs_ref, bias_ref, cell_ref, lat_ref, dout_ref, wq_ref, wo_ref,
+    recv_ref, rmeta_ref, q_ref, back_ref,
+    foot_v, obs_v, bias_v, cell_v, lat_v, dout_v, wq_v, wo_v, q_v, back_v,
+    stage, mstage, osend, omsend, foot_s, marks_s, sem_in, sem_out, sem_core, sem_chip,
+):
+    lat, lon = lax.axis_index("lat"), lax.axis_index("lon")
+    core = lax.rem(lat, 2)
+    y, z, x = lat // 2, lon // 4, lax.rem(lon, 4)
+    loads = []
+    for i, (src, dst) in enumerate((
+        (foot_ref, foot_v), (obs_ref, obs_v), (bias_ref, bias_v), (cell_ref, cell_v),
+        (lat_ref, lat_v), (wq_ref, wq_v), (dout_ref, dout_v), (wo_ref, wo_v),
+    )):
+        loads.append(pltpu.make_async_copy(src, dst, sem_in.at[i]))
+        loads[-1].start()
+
+    ys = [lax.rem(y + d, 4) for d in range(4)]
+    lons = [lax.rem(z + d // 4, 4) * 4 + lax.rem(x + d % 4, 4) for d in range(16)]
+    chips = []
+    for k in range(1, 64):
+        cy, cl = ys[k // 16], lons[k % 16]
+        chips.append((cy * 16 + cl, {"lat": cy * 2 + core, "lon": cl}))
+    sibling = {"lat": y * 2 + 1 - core, "lon": lon}
+    my_chip = y * 16 + lon
+    barrier = pltpu.get_barrier_semaphore()
+    pl.semaphore_signal(barrier, inc=1, device_id=sibling, device_id_type=MESH)
+    for chip, where in chips:
+        pl.semaphore_signal(barrier, inc=1, device_id=where, device_id_type=MESH)
+
+    foot_s[...] = jnp.full((16, 128), -1.0, F32)
+    marks_s[...] = jnp.zeros((128, 1280), F32)
+    for load in loads[:4]:
+        load.wait()
+    foot_s[0:4, 0:32] = foot_v[...].astype(F32)
+    for rank in range(CAP):
+        lane, at = rank * OBS, rank * 640
+        marks_s[lane : lane + OBS, at : at + 32] = bias_v[...].astype(F32)
+        for f in range(4):
+            lane, at = (CAP + rank) * OBS, rank * 640 + (1 + f) * 128
+            marks_s[lane : lane + OBS, at : at + 32] = cell_v[f].astype(F32) - float(GROUPS)
+    foot = foot_s[...]
+    marks = marks_s[...].astype(BF16)
+    r, c = iota((128, 128), 0), iota((128, 128), 1)
+    upper = hot(r < c)
+    widen = hot(iota((128, 256), 1) // OBS == iota((128, 256), 0))
+    keep = iota((1024, 256), 0) % OBS == iota((1024, 256), 1) % OBS
+
+    def slots_of(to_core):
+        tile = (r // 32) * 32 + to_core * 16 + (r // CAP) % 16
+        hit = jnp.zeros((128, 128), F32)
+        for f in range(4):
+            hit = hit + jnp.where(foot[f : f + 1, :] == tile.astype(F32), 1.0, 0.0)
+        sel = hit * jnp.where(dot(hit.astype(BF16), upper) == (r % CAP).astype(F32), 1.0, 0.0)
+        blocks = dot(sel.astype(BF16), widen)
+        spread = jnp.broadcast_to(blocks[:, None, :], (128, OBS, 256)).reshape(1024, 256)
+        rows = dot(jnp.where(keep, spread, 0.0).astype(BF16), obs_v[...]).astype(BF16)
+        tile = iota((64, 128), 0)
+        tile = ((tile // 16) * 32 + to_core * 16 + tile % 16).astype(F32)
+        hits = [jnp.where(foot[f : f + 1, :] == tile, 1.0, 0.0) for f in range(4)]
+        any_hit = hits[0] + hits[1] + hits[2] + hits[3]
+        order = dot(any_hit.astype(BF16), upper)
+        left = []
+        for rank in range(CAP):
+            chosen = any_hit * jnp.where(order == float(rank), 1.0, 0.0)
+            left += [chosen] + [chosen * hits[f] for f in range(4)]
+        meta = dot_nt(jnp.concatenate(left, axis=1).astype(BF16), marks)
+        return rows.reshape(64, 16, CH), meta.reshape(64, 1, 128)
+
+    osend[...], omsend[...] = slots_of(1 - core)
+    pl.semaphore_wait(barrier, 64)
+
+    def copy(src, dst, sems, where):
+        return pltpu.make_async_remote_copy(
+            src_ref=src, dst_ref=dst, send_sem=sems.at[0], recv_sem=sems.at[1], device_id=where, device_id_type=MESH,
+        )
+
+    swap = [copy(osend, stage.at[core], sem_core.at[0], sibling), copy(omsend, mstage.at[core], sem_core.at[1], sibling)]
+    for part in swap:
+        part.start()
+    stage[core], mstage[core] = slots_of(core)
+    for part in swap:
+        part.wait_recv()
+    for chip, where in chips:
+        copy(stage.at[:, chip], recv_ref.at[:, my_chip], sem_chip.at[0], where).start()
+        copy(mstage.at[:, chip], rmeta_ref.at[:, my_chip], sem_chip.at[1], where).start()
+    stores = [
+        pltpu.make_async_copy(stage.at[:, my_chip], recv_ref.at[:, my_chip], sem_out.at[0]),
+        pltpu.make_async_copy(mstage.at[:, my_chip], rmeta_ref.at[:, my_chip], sem_out.at[1]),
+    ]
+    for store in stores:
+        store.start()
+
+    loads[4].wait()
+    loads[5].wait()
+    q_v[...] = (dot(lat_v[...], wq_v[...]).astype(BF16).astype(F32) * 0.125).astype(BF16)
+    stores.append(pltpu.make_async_copy(q_v, q_ref, sem_out.at[2]))
+    stores[-1].start()
+    loads[6].wait()
+    loads[7].wait()
+    back_v[...] = dot_nt(dout_v[...], wo_v[...]).astype(BF16)
+    stores.append(pltpu.make_async_copy(back_v, back_ref, sem_out.at[3]))
+    stores[-1].start()
+
+    whole = copy(stage.at[:, 0:63], recv_ref.at[:, 0:63], sem_chip.at[0], sibling)
+    marks = copy(mstage.at[:, 0:63], rmeta_ref.at[:, 0:63], sem_chip.at[1], sibling)
+    whole.wait_recv()
+    marks.wait_recv()
+    whole.wait_send()
+    marks.wait_send()
+    for part in swap:
+        part.wait_send()
+    for store in stores:
+        store.wait()
 
 
 def tile_kernel(
-    recv_ref, lat_ref, dout_ref, wobs_ref, wkv_ref, wq_ref, wo_ref,
-    upd_ref, dlat_ref, grads_ref,
-    q_s, back_s, rows_s, slope_s, enc_s, kv_s, bias_s, attn_s, attnt_s, dq_s, meta_sm,
+    recv_ref, rmeta_ref, q_ref, back_ref, lat_ref, dout_ref, wobs_ref, wkv_ref, wq_ref, wo_ref,
+    upd_ref, dlat_ref, main_ref, part_ref, rows_ref, slope_ref, dkv_ref,
+    rows_s, slope_s, enct_s, kv_s, bias_s, attn_s, attnt_s, dq_s, sums_s, main_v, part_v, upd_v, dlat_v, meta_sm,
+    recv_v, rmeta_v, q_s, back_s, lat_v, dout_v, wobs_v, wkv_v, wq_v, wo_v, sem_in, sem_blk, sem_out,
 ):
-    me = lax.axis_index(("lat", "lon"))
-
-    take = jnp.where(iota((16, 128), 0) == iota((16, 128), 1), 1.0, 0.0).astype(BF16)
-    meta = dot_nt(take, recv_ref[:, CH:])
-    mine = (me + 1).astype(F32)
-    cell = jnp.full((1, ROWS), float(GROUPS), F32)
-    for f in range(4):
-        cell = jnp.where(meta[5 + f : 6 + f, :] == mine, meta[1 + f : 2 + f, :], cell)
-    cell = jnp.concatenate([cell[:, i * 128 : (i + 1) * 128] for i in range(16)], axis=0)
+    loads = []
+    for i, (src, dst) in enumerate((
+        (rmeta_ref, rmeta_v), (recv_ref, recv_v), (wobs_ref, wobs_v), (wkv_ref, wkv_v), (q_ref, q_s), (back_ref, back_s),
+        (lat_ref, lat_v), (dout_ref, dout_v), (wq_ref, wq_v), (wo_ref, wo_v),
+    )):
+        loads.append(pltpu.make_async_copy(src, dst, sem_in.at[i]))
+        loads[-1].start()
+
+    def block_out(b, i):
+        src, dst = ((rows_s, rows_ref), (slope_s, slope_ref), (kv_s, dkv_ref))[i]
+        at = pl.ds(pl.multiple_of(b * KB, KB), KB)
+        return pltpu.make_async_copy(src.at[at, :], dst.at[at, :], sem_blk.at[i, b])
+
+    loads[0].wait()
+    r, c = iota((128, 128), 0), iota((128, 128), 1)
+    marks = rmeta_v[...].astype(BF16)
+    own_lane = r % 8 == c // 16
+    chunk = jnp.where(iota((16, 128), 0) == iota((16, 128), 1) // 8, 1.0, 0.0).astype(BF16)
+
+    def laned(first_lane):
+        lanes = dot(marks, jnp.where(r == c % 16 + first_lane, 1.0, 0.0).astype(BF16))
+        return dot(chunk, jnp.where(own_lane, lanes, 0.0).astype(BF16))
+
+    bias_row = laned(0)
+    cell = laned(16) + float(GROUPS)
+    bias_row = jnp.concatenate([bias_row[i : i + 1, :] for i in range(16)], axis=1)
+    kind = iota((16, ROWS), 0)
+    extra = jnp.where(kind == 0, bias_row, jnp.where(kind == 1, 1.0, 0.0)).astype(BF16)
     inside = jnp.concatenate([jnp.where(cell == float(g), 1.0, 0.0) for g in range(GROUPS)], axis=0)
-    r, c = iota((128, 128), 0), iota((128, 128), 1)
     upto = jnp.where(r <= c, 1.0, 0.0).astype(BF16)
     prefix = dot(inside.astype(BF16), upto)
     total = jnp.broadcast_to(prefix[:, 127:128], (128, 128)).astype(BF16)
@@ -105,9 +229,6 @@
         meta_sm[1, g] = jnp.max(nblk[g * 16 : g * 16 + 8, :]).astype(jnp.int32)
     blocks = meta_sm[0, GROUPS - 1] + meta_sm[1, GROUPS - 1]
 
-    q_s[...] = (dot(lat_ref[...], wq_ref[...]).astype(BF16).astype(F32) * 0.125).astype(BF16)
-    back_s[...] = dot_nt(dout_ref[...], wo_ref[...]).astype(BF16)
-
     lane_pos = [jnp.broadcast_to(pos[i : i + 1, :], (16, 128)) for i in range(16)]
     row_id = iota((KB, 128), 0).astype(F32).astype(BF16)
 
@@ -119,19 +240,30 @@
             rel = jnp.clip(lane_pos[i] - base, -1.0, float(KB)).astype(BF16)
             rel = jnp.concatenate([rel] * (KB // 16), axis=0)
             cols.append(jnp.where(row_id == rel, jnp.ones((), BF16), jnp.zeros((), BF16)))
-        got = dot(jnp.concatenate(cols, axis=1), recv_ref[...])
-        rows = got[:, :CH].astype(BF16)
-        bias = jnp.where(got[:, CH + 15 : CH + 16] > 0.5, got[:, CH : CH + 1], NEG)
+        choose = jnp.concatenate(cols, axis=1)
+        rows = dot(choose, recv_v[...]).astype(BF16)
+        side = dot_nt(choose, extra)
+        bias = jnp.where(side[:, 1:2] > 0.5, side[:, 0:1], NEG)
         bias_s[pl.ds(r0, KB), :] = jnp.broadcast_to(bias, (KB, 128))
         rows_s[pl.ds(r0, KB), :] = rows
-        value, slope = gelu_parts(dot(rows, wobs_ref[...]))
+        value, slope = gelu_parts(dot(rows, wobs_v[...]))
         enc = value.astype(BF16)
-        slope_s[pl.ds(r0, KB), :] = slope
-        enc_s[pl.ds(r0, KB), :] = enc
-        kv_s[pl.ds(r0, KB), :] = dot(enc, wkv_ref[...]).astype(BF16)
+        slope_s[pl.ds(r0, KB), :] = slope.astype(BF16)
+        enct_s[:, pl.ds(r0, KB)] = enc.T
+        kv_s[pl.ds(r0, KB), :] = dot(enc, wkv_v[...]).astype(BF16)
+
+        @pl.when(b < LEAD)
+        def _():
+            for i in range(2):
+                block_out(b, i).start()
+
         return carry
 
-    lax.fori_loop(0, blocks, encode, 0)
+    for load in loads[1:4]:
+        load.wait()
+    lax.fori_loop(0, jnp.maximum(blocks, LEAD), encode, 0)
+    for load in loads[4:6]:
+        load.wait()
 
     lane_head = iota((GCELLS, 256), 1) // 64
 
@@ -224,88 +356,428 @@
                 zero = jnp.zeros((256, GCELLS), F32)
                 put(half, *lax.fori_loop(0, nb, third_pass, (zero, zero)))
 
+        def send_block(b, carry):
+            block_out(b, 2).start()
+            return carry
+
+        lax.fori_loop(jnp.minimum(start, LEAD), jnp.minimum(start + nb, LEAD), send_block, 0)
         return carry
 
     lax.fori_loop(0, GROUPS, group, 0)
 
+    def send_empty(b, carry):
+        block_out(b, 2).start()
+        return carry
+
+    lax.fori_loop(jnp.minimum(blocks, LEAD), LEAD, send_empty, 0)
+
+    for load in loads[6:]:
+        load.wait()
     attn, dq = attn_s[...], dq_s[...]
-    upd_ref[...] = (lat_ref[...].astype(F32) + dot(attn, wo_ref[...])).astype(BF16)
-    dlat_ref[...] = (dout_ref[...].astype(F32) + dot_nt(dq, wq_ref[...])).astype(BF16)
-    grads_ref[1280:1792, :] = dot_tn(lat_ref[...], dq)
+    outs = []
+
+    def put_out(src, dst):
+        outs.append(pltpu.make_async_copy(src, dst, sem_out.at[len(outs)]))
+        outs[-1].start()
+
+    main_v[0, 0:512, :] = dot_tn(lat_v[...], dq).astype(BF16)
     attnt = jnp.concatenate([attnt_s[g] for g in range(GROUPS)], axis=1)
-    grads_ref[1792:2304, :] = dot(attnt, dout_ref[...])
-
-    grads_ref[0:1280, :] = jnp.zeros((1280, D), F32)
-
-    def encoder_grads(b, carry):
-        r0 = pl.multiple_of(b * KB, KB)
-        dkv = kv_s[pl.ds(r0, KB), :]
-        denc = dot_nt(dkv, wkv_ref[...])
-        dpre = (denc * slope_s[pl.ds(r0, KB), :]).astype(BF16)
-        grads_ref[0:256, :] += dot_tn(rows_s[pl.ds(r0, KB), :], dpre)
-        part = dot_tn(enc_s[pl.ds(r0, KB), :], dkv)
-        grads_ref[256:768, :] += part[:, :D]
-        grads_ref[768:1280, :] += part[:, D:]
-        return carry
-
-    lax.fori_loop(0, blocks, encoder_grads, 0)
+    main_v[1, 0:512, :] = dot(attnt, dout_v[...]).astype(BF16)
+
+    @pl.when(blocks <= LEAD)
+    def _():
+        for i in range(4):
+            tile = dot(enct_s[:, 0:ROWS], kv_s[0:ROWS, i * 256 : (i + 1) * 256])
+            main_v[i // 2, 512:1024, i % 2 * 256 : i % 2 * 256 + 256] = tile.astype(BF16)
+        part_v[...] = jnp.zeros((CH, D), BF16)
+
+    @pl.when(blocks > LEAD)
+    def _():
+        for i in range(4):
+            sums_s[0:512, i * 256 : (i + 1) * 256] = dot(enct_s[:, 0:ROWS], kv_s[0:ROWS, i * 256 : (i + 1) * 256])
+        sums_s[512:768, 0:512] = jnp.zeros((CH, D), F32)
+
+        def encoder_grads(b, carry):
+            r0 = pl.multiple_of(b * KB, KB)
+            dkv = kv_s[pl.ds(r0, KB), :]
+            dpre = (dot_nt(dkv, wkv_v[...]) * slope_s[pl.ds(r0, KB), :].astype(F32)).astype(BF16)
+            sums_s[0:512, :] += dot(enct_s[:, pl.ds(r0, KB)], dkv)
+            sums_s[512:768, 0:512] += dot_tn(rows_s[pl.ds(r0, KB), :], dpre)
+            return carry
+
+        lax.fori_loop(LEAD, blocks, encoder_grads, 0)
+        for h in range(2):
+            main_v[h, 512:1024, :] = sums_s[0:512, h * 512 : (h + 1) * 512].astype(BF16)
+        part_v[...] = sums_s[512:768, 0:512].astype(BF16)
+
+    put_out(main_v, main_ref)
+    put_out(part_v, part_ref)
+    upd_v[...] = (lat_v[...].astype(F32) + dot(attn, wo_v[...])).astype(BF16)
+    put_out(upd_v, upd_ref)
+    dlat_v[...] = (dout_v[...].astype(F32) + dot_nt(dq, wq_v[...])).astype(BF16)
+    put_out(dlat_v, dlat_ref)
+
+    for i in range(3):
+        for b in range(LEAD):
+            block_out(b, i).wait()
+    for out in outs:
+        out.wait()
+
+
+ORDER = ("x", "y", "z")
+JOBS = (("main", 0, 384, 0), ("main", 384, 320, 1), ("main", 704, 320, 2), ("obs", 0, 64, 1), ("obs", 64, 64, 2))
+
+
+def peer(step_axis, k):
+    lat, lon = lax.axis_index("lat"), lax.axis_index("lon")
+    y, core, z, x = lat // 2, lat % 2, lon // 4, lon % 4
+    if step_axis == "x":
+        x = (x + k) % 4
+    elif step_axis == "y":
+        y = (y + k) % 4
+    elif step_axis == "z":
+        z = (z + k) % 4
+    else:
+        core = 1 - core
+    return {"lat": y * 2 + core, "lon": z * 4 + x}
+
+
+def place_on(step_axis):
+    lat, lon = lax.axis_index("lat"), lax.axis_index("lon")
+    return {"x": lon % 4, "y": lat // 2, "z": lon // 4}[step_axis]
+
+
+class Job:
+    def __init__(self, source, mine, half, start, rows, turn, bufs, sems):
+        self.source, self.mine, self.start, self.rows, self.piece = source, mine, start, rows, rows // 4
+        self.axes = [ORDER[(turn + i) % 3] for i in range(3)]
+        self.core_recv, self.src1, self.recv1, self.src2, self.recv2, self.buf3, self.full, self.other = bufs
+        self.sems, self.half, self.phase, self.sent = sems, half, -1, []
+
+    def describe(self, src, dst, axis, k):
+        return pltpu.make_async_remote_copy(
+            src_ref=src, dst_ref=dst, send_sem=self.sems.at[self.phase, 0], recv_sem=self.sems.at[self.phase, 1],
+            device_id=peer(axis, k), device_id_type=MESH,
+        )
+
+    def swap(self):
+        self.phase += 1
+        at = self.source.at[1 - self.half, pl.ds(self.start, self.rows), :]
+        copy = self.describe(at, self.core_recv, "core", 1)
+        copy.start()
+        self.sent.append(copy)
+
+    def around(self, axis, src_of, dst_of, whole):
+        self.phase += 1
+        for k in range(1, 4):
+            self.describe(src_of(k), dst_of(k), axis, k).start()
+        self.sent.append(self.describe(whole, whole, axis, 1))
+
+    def arrived(self):
+        self.sent[-1].wait_recv()
+
+    def scatter1(self):
+        self.arrived()
+        own = self.mine[self.half, self.start : self.start + self.rows, :].astype(F32)
+        total = (own + self.core_recv[...].astype(F32)).astype(BF16)
+        for j in range(4):
+            self.src1[j] = total[j * self.piece : (j + 1) * self.piece, :]
+        at = place_on(self.axes[0])
+        self.around(
+            self.axes[0], lambda k: self.src1.at[lax.rem(at + k, 4)], lambda k: self.recv1.at[k - 1], self.recv1
+        )
+
+    def scatter2(self):
+        self.arrived()
+        total = self.src1[place_on(self.axes[0])].astype(F32)
+        for k in range(3):
+            total = total + self.recv1[k].astype(F32)
+        for j in range(4):
+            self.src2[j] = total[:, j * 128 : (j + 1) * 128].astype(BF16)
+        at = place_on(self.axes[1])
+        self.around(
+            self.axes[1], lambda k: self.src2.at[lax.rem(at + k, 4)], lambda k: self.recv2.at[k - 1], self.recv2
+        )
+
+    def exchange3(self):
+        self.arrived()
+        total = self.src2[place_on(self.axes[1])].astype(F32)
+        for k in range(3):
+            total = total + self.recv2[k].astype(F32)
+        self.buf3[0] = total.astype(BF16)
+        self.around(self.axes[2], lambda k: self.buf3.at[0], lambda k: self.buf3.at[k], self.buf3.at[1:4])
+
+    def gather2(self):
+        self.arrived()
+        at = place_on(self.axes[2])
+        total = self.buf3[at].astype(F32)
+        for s in range(1, 4):
+            total = total + self.buf3[lax.rem(at + 4 - s, 4)].astype(F32)
+        i, j = place_on(self.axes[0]), place_on(self.axes[1])
+        self.full[i, j] = total.astype(BF16)
+        mine = self.full.at[i, j]
+        self.around(self.axes[1], lambda k: mine, lambda k: mine, self.recv2)
+
+    def gather1(self):
+        self.arrived()
+        mine = self.full.at[place_on(self.axes[0])]
+        self.around(self.axes[0], lambda k: mine, lambda k: mine, self.recv1)
+
+    def share(self, out_ref):
+        self.arrived()
+        self.phase += 1
+        copy = self.describe(self.full, self.other, "core", 1)
+        copy.start()
+        self.sent.append(copy)
+        self.write(out_ref, self.full, self.half)
+
+    def write(self, out_ref, block, half):
+        for i in range(4):
+            for j in range(4):
+                out_ref[half, self.start + i * self.piece : self.start + (i + 1) * self.piece, j * 128 : (j + 1) * 128] = block[i, j]
+
+    def end(self, out_ref):
+        self.arrived()
+        self.write(out_ref, self.other, 1 - self.half)
+
+    def settle(self):
+        for copy in self.sent:
+            copy.wait_send()
+
+
+def sum_kernel(
+    main_ref, part_ref, rows_ref, slope_ref, dkv_ref, wkv_ref,
+    omain_ref, oobs_ref,
+    main_v, part_v, rows_v, slope_v, dkv_v, wkv_v, gobs_v, dpre_s, omain_v, oobs_v, sem_in, sem_out, *scratch,
+):
+    half = lax.rem(lax.axis_index("lat"), 2)
+    loads = []
+    for i, (src, dst) in enumerate((
+        (main_ref, main_v), (dkv_ref, dkv_v), (wkv_ref, wkv_v),
+        (slope_ref, slope_v), (rows_ref, rows_v), (part_ref, part_v),
+    )):
+        loads.append(pltpu.make_async_copy(src, dst, sem_in.at[i]))
+        loads[-1].start()
+    barrier = pltpu.get_barrier_semaphore()
+    pl.semaphore_signal(barrier, inc=1, device_id=peer("core", 1), device_id_type=MESH)
+    for axis in ORDER:
+        for k in range(1, 4):
+            pl.semaphore_signal(barrier, inc=1, device_id=peer(axis, k), device_id_type=MESH)
+    sources = {"main": (main_ref, main_v), "obs": (gobs_v, gobs_v)}
+    outs = {"main": omain_v, "obs": oobs_v}
+    jobs = {"main": [], "obs": []}
+    for i, (name, start, rows, turn) in enumerate(JOBS):
+        bufs = scratch[9 * i : 9 * i + 8]
+        jobs[name].append(Job(*sources[name], half, start, rows, turn, bufs, scratch[9 * i + 8]))
+
+    def step(name, what):
+        for job in jobs[name]:
+            if what in ("share", "end"):
+                getattr(job, what)(outs[name])
+            else:
+                getattr(job, what)()
+
+    def through_encoder(i):
+        at = slice(i * 512, (i + 1) * 512)
+        denc = dot_nt(dkv_v[at, :], wkv_v[...])
+        dpre_s[at, :] = (denc * slope_v[at, :].astype(F32)).astype(BF16)
+
+    pl.semaphore_wait(barrier, 10)
+    step("main", "swap")
+    for load in loads:
+        load.wait()
+    through_encoder(0)
+    step("main", "scatter1")
+    through_encoder(1)
+    through_encoder(2)
+    step("main", "scatter2")
+    through_encoder(3)
+    total = dot_tn(rows_v[...], dpre_s[...]) + part_v[...].astype(F32)
+    gobs_v[0] = total[0:128].astype(BF16)
+    gobs_v[1] = total[128:256].astype(BF16)
+    step("obs", "swap")
+    step("main", "exchange3")
+    step("obs", "scatter1")
+    step("main", "gather2")
+    step("obs", "scatter2")
+    step("main", "gather1")
+    step("obs", "exchange3")
+    step("obs", "gather2")
+    step("main", "share")
+    step("obs", "gather1")
+    step("main", "end")
+    store = pltpu.make_async_copy(omain_v, omain_ref, sem_out.at[0])
+    store.start()
+    step("obs", "share")
+    step("obs", "end")
+    last = pltpu.make_async_copy(oobs_v, oobs_ref, sem_out.at[1])
+    last.start()
+    for name in jobs:
+        for job in jobs[name]:
+            job.settle()
+    store.wait()
+    last.wait()
+
+
+def widen_kernel(main_ref, gobs_ref, obs_ref, kv_ref, q_ref, o_ref):
+    obs_ref[...] = gobs_ref[0].astype(F32)
+    q_ref[...] = main_ref[0, 0].astype(F32)
+    o_ref[...] = main_ref[1, 0].astype(F32)
+    for h in range(2):
+        kv_ref[:, h * D : (h + 1) * D] = main_ref[h, 1].astype(F32)
+
+
+def sum_grads(main, part, rows, slope, dkv, w_kv):
+    far = pl.BlockSpec(memory_space=pltpu.HBM)
+    dma = pltpu.SemaphoreType.DMA
+    scratch = []
+    for _, _, n, _ in JOBS:
+        piece = n // 4
+        scratch += [
+            pltpu.VMEM((n, D), BF16),
+            pltpu.VMEM((4, piece, D), BF16),
+            pltpu.VMEM((3, piece, D), BF16),
+            pltpu.VMEM((4, piece, 128), BF16),
+            pltpu.VMEM((3, piece, 128), BF16),
+            pltpu.VMEM((4, piece, 128), BF16),
+            pltpu.VMEM((4, 4, piece, 128), BF16),
+            pltpu.VMEM((4, 4, piece, 128), BF16),
+            dma((7, 2)),
+        ]
+    return pl.pallas_call(
+        sum_kernel,
+        out_shape=[jax.ShapeDtypeStruct((2, 2 * D, D), BF16), jax.ShapeDtypeStruct((2, 128, D), BF16)],
+        in_specs=[far] * 6,
+        out_specs=[far] * 2,
+        scratch_shapes=[
+            pltpu.VMEM((2, 2 * D, D), BF16),
+            pltpu.VMEM((CH, D), BF16),
+            pltpu.VMEM((ROWS, CH), BF16),
+            pltpu.VMEM((ROWS, D), BF16),
+            pltpu.VMEM((ROWS, 2 * D), BF16),
+            pltpu.VMEM((D, 2 * D), BF16),
+            pltpu.VMEM((2, 128, D), BF16),
+            pltpu.VMEM((ROWS, D), BF16),
+            pltpu.VMEM((2, 2 * D, D), BF16),
+            pltpu.VMEM((2, 128, D), BF16),
+            dma((6,)),
+            dma((2,)),
+        ] + scratch,
+        compiler_params=pltpu.CompilerParams(
+            collective_id=1, has_side_effects=True, vmem_limit_bytes=VMEM_LIMIT
+        ),
+        name="sum_grads",
+    )(main, part, rows, slope, dkv, w_kv)
 
 
 def body(latents, d_out, observations, obs_bias, footprint, obs_cell, w_obs, w_kv, w_q, w_o):
-    blocks = observations.shape[0]
-    rows = blocks * OBS
-    foot = jnp.pad(footprint.T, ((0, 4), (0, 128 - blocks)), constant_values=-1)
-    one = jnp.ones((rows, 1), BF16)
-    meta = jnp.concatenate(
-        [
-            obs_bias.reshape(rows, 1),
-            obs_cell.transpose(0, 2, 1).reshape(rows, 4).astype(BF16),
-            jnp.broadcast_to(footprint[:, None, :] + 1, (blocks, OBS, 4)).reshape(rows, 4).astype(BF16),
-            jnp.zeros((rows, 6), BF16),
-            one,
-            jnp.zeros((rows, 112), BF16),
+    vmem = pl.BlockSpec(memory_space=pltpu.VMEM)
+    dma = pltpu.SemaphoreType.DMA
+    far = pl.BlockSpec(memory_space=pltpu.HBM)
+    recv, rmeta, q, back = pl.pallas_call(
+        exchange_kernel,
+        out_shape=(
+            jax.ShapeDtypeStruct((2, 64, 16, CH), BF16),
+            jax.ShapeDtypeStruct((2, 64, 1, 128), F32),
+            jax.ShapeDtypeStruct((CELLS, D), BF16),
+            jax.ShapeDtypeStruct((CELLS, D), BF16),
+        ),
+        in_specs=[far] * 8,
+        out_specs=[far] * 4,
+        scratch_shapes=[
+            pltpu.VMEM((4, 32), jnp.int32),
+            pltpu.VMEM((32 * OBS, CH), BF16),
+            pltpu.VMEM((OBS, 32), BF16),
+            pltpu.VMEM((4, OBS, 32), jnp.int32),
+            pltpu.VMEM((CELLS, D), BF16),
+            pltpu.VMEM((CELLS, D), BF16),
+            pltpu.VMEM((D, D), BF16),
+            pltpu.VMEM((D, D), BF16),
+            pltpu.VMEM((CELLS, D), BF16),
+            pltpu.VMEM((CELLS, D), BF16),
+            pltpu.VMEM((2, 64, 16, CH), BF16),
+            pltpu.VMEM((2, 64, 1, 128), F32),
+            pltpu.VMEM((64, 16, CH), BF16),
+            pltpu.VMEM((64, 1, 128), F32),
+            pltpu.VMEM((16, 128), F32),
+            pltpu.VMEM((128, 1280), F32),
+            dma((8,)),
+            dma((4,)),
+            dma((2, 2)),
+            dma((2, 2)),
         ],
-        axis=1,
+        compiler_params=pltpu.CompilerParams(
+            collective_id=0, has_side_effects=True, vmem_limit_bytes=VMEM_LIMIT
+        ),
+        name="exchange",
+    )(
+        footprint.T, observations.reshape(-1, CH), obs_bias.T, obs_cell.transpose(1, 2, 0),
+        latents, d_out, w_q, w_o,
     )
-    wide = jnp.concatenate([observations.reshape(rows, CH), meta], axis=1)
-    vmem = pl.BlockSpec(memory_space=pltpu.VMEM)
-    payload = pl.pallas_call(
-        pack_kernel,
-        out_shape=jax.ShapeDtypeStruct((ROWS, WIDE), BF16),
-        in_specs=[vmem] * 2,
-        out_specs=vmem,
-        compiler_params=pltpu.CompilerParams(vmem_limit_bytes=40 << 20),
-        name="pack",
-    )(foot, wide)
-    recv = lax.all_to_all(payload, ("lat", "lon"), split_axis=0, concat_axis=0, tiled=True)
-    upd, dlat, grads = pl.pallas_call(
+    upd, dlat, main, part, rows, slope, dkv = pl.pallas_call(
         tile_kernel,
         out_shape=(
             jax.ShapeDtypeStruct((CELLS, D), BF16),
             jax.ShapeDtypeStruct((CELLS, D), BF16),
-            jax.ShapeDtypeStruct((2304, D), F32),
+            jax.ShapeDtypeStruct((2, 2 * D, D), BF16),
+            jax.ShapeDtypeStruct((CH, D), BF16),
+            jax.ShapeDtypeStruct((ROWS, CH), BF16),
+            jax.ShapeDtypeStruct((ROWS, D), BF16),
+            jax.ShapeDtypeStruct((ROWS, 2 * D), BF16),
         ),
-        in_specs=[vmem] * 7,
-        out_specs=(vmem, vmem, vmem),
+        in_specs=[far] * 10,
+        out_specs=[far] * 7,
         scratch_shapes=[
-            pltpu.VMEM((CELLS, D), BF16),
-            pltpu.VMEM((CELLS, D), BF16),
             pltpu.VMEM((MAXB * KB, CH), BF16),
-            pltpu.VMEM((MAXB * KB, D), F32),
             pltpu.VMEM((MAXB * KB, D), BF16),
+            pltpu.VMEM((D, MAXB * KB), BF16),
             pltpu.VMEM((MAXB * KB, 2 * D), BF16),
             pltpu.VMEM((MAXB * KB, 128), F32),
             pltpu.VMEM((CELLS, D), BF16),
             pltpu.VMEM((GROUPS, D, GCELLS), BF16),
             pltpu.VMEM((CELLS, D), BF16),
+            pltpu.VMEM((768, 2 * D), F32),
+            pltpu.VMEM((2, 2 * D, D), BF16),
+            pltpu.VMEM((CH, D), BF16),
+            pltpu.VMEM((CELLS, D), BF16),
+            pltpu.VMEM((CELLS, D), BF16),
             pltpu.SMEM((2, GROUPS), jnp.int32),
+            pltpu.VMEM((ROWS, CH), BF16),
+            pltpu.VMEM((DEV, 128), F32),
+            pltpu.VMEM((CELLS, D), BF16),
+            pltpu.VMEM((CELLS, D), BF16),
+            pltpu.VMEM((CELLS, D), BF16),
+            pltpu.VMEM((CELLS, D), BF16),
+            pltpu.VMEM((CH, D), BF16),
+            pltpu.VMEM((D, 2 * D), BF16),
+            pltpu.VMEM((D, D), BF16),
+            pltpu.VMEM((D, D), BF16),
+            dma((10,)),
+            dma((3, LEAD)),
+            dma((4,)),
         ],
-        compiler_params=pltpu.CompilerParams(vmem_limit_bytes=60 << 20),
+        compiler_params=pltpu.CompilerParams(vmem_limit_bytes=VMEM_LIMIT),
         name="tile",
-    )(recv, latents, d_out, w_obs, w_kv, w_q, w_o)
-    grads = lax.psum(grads, ("lat", "lon"))
-    gkv = jnp.concatenate([grads[256:768], grads[768:1280]], axis=1)
-    return upd, dlat, grads[0:256], gkv, grads[1280:1792], grads[1792:2304]
+    )(recv.reshape(ROWS, CH), rmeta.reshape(DEV, 128), q, back, latents, d_out, w_obs, w_kv, w_q, w_o)
+    gmain, gobs = sum_grads(main, part, rows, slope, dkv, w_kv)
+    gobs, gkv, gq, go = pl.pallas_call(
+        widen_kernel,
+        grid=(4,),
+        out_shape=[jax.ShapeDtypeStruct(x.shape, F32) for x in (w_obs, w_kv, w_q, w_o)],
+        in_specs=[
+            pl.BlockSpec((2, 2, 128, D), lambda i: (0, 0, i, 0)),
+            pl.BlockSpec((1, 64, D), lambda i: (i // 2, i % 2, 0)),
+        ],
+        out_specs=[
+            pl.BlockSpec((64, D), lambda i: (i, 0)),
+            pl.BlockSpec((128, 2 * D), lambda i: (i, 0)),
+            pl.BlockSpec((128, D), lambda i: (i, 0)),
+            pl.BlockSpec((128, D), lambda i: (i, 0)),
+        ],
+        compiler_params=pltpu.CompilerParams(vmem_limit_bytes=VMEM_LIMIT),
+        name="widen",
+    )(gmain.reshape(2, 2, D, D), gobs)
+    return upd, dlat, gobs, gkv, gq, go
 
 
 def solution(mesh):

time: 263 us -> 109 us (0.41)
  waiting for transfers between devices: 158 us -> 0 us
  Pallas kernels: 43.7 us -> 108 us
  blocking collectives: 35.5 us -> 0 us
  between operations: 14.1 us -> 0.66 us
  local copies, waits for them, and re-layouts: 8.94 us -> 0 us
  other arithmetic: 2.92 us -> 0 us
    psum x1 -> x0, waiting for transfers between devices: 158 us -> none  [body(): grads = lax.psum(grads, ('lat', 'lon'))]
    pallas_call x1 -> x3, Pallas kernels: 0.95 us -> 74.1 us  [the longest x1 39.6 us: sum_grads(): pl.pallas_call(sum_kernel, out_shape=[jax.ShapeDtypeStruct((2, 2 * D, D),...]
    all_to_all x1 -> x0, blocking collectives: 35.5 us -> none  [body(): lax.all_to_all(payload, ('lat', 'lon'), split_axis=0, concat_axis=0, tile...]
    pallas_call x1, Pallas kernels: 42.8 us -> 33.9 us  [body(): pl.pallas_call(tile_kernel, out_shape=(jax.ShapeDtypeStruct((CELLS, D), B...]
    slice x2 -> x0, local copies, waits for them, and re-layouts: 6 us -> none  [body(): return (upd, dlat, grads[0:256], gkv, grads[1280:1792], grads[1792:2304])]
  transfers between devices with their start and end apart: 1 -> 0, of which waited for: 1 -> 0; matrix products, arithmetic and copies ran while one was open for 0% -> 0% of each run, Pallas kernels for 0% -> 0%
where the time goes in v3:
time: 109 us
  Pallas kernels  108 us (99%)
    pallas_call x1, Pallas kernels, sum_grads(): pl.pallas_call(sum_kernel, out_shape=[jax.ShapeDtypeStruct((2, 2 * D, D),...  39.6 us
    pallas_call x1, Pallas kernels, body(): pl.pallas_call(tile_kernel, out_shape=(jax.ShapeDtypeStruct((CELLS, D), B...  33.9 us
    pallas_call x1, Pallas kernels, body(): pl.pallas_call(exchange_kernel, out_shape=(jax.ShapeDtypeStruct((2, 64, 1...  30.2 us
    pallas_call x1, Pallas kernels, body(): pl.pallas_call(widen_kernel, grid=(4,), out_shape=[jax.ShapeDtypeStruct(x...  4.29 us

profile of v3, /device:TPU:1, one launch (start us, length us, event | category | flops | bytes accessed | tf_op | source)
XLA Modules:
  0.0 108.6 jit_solution(13895942171010761495)
XLA Ops:
  0.6 30.2 %exchange.1 = (bf16[2,64,16,256]{3,2,1,0:T(8,128)(2,1)}, f32[2,64,1,128]{3,2,1,0:T(1,128)}, bf16[1024,512]{1,0:T(8,128)(2,1)}, bf16[1024,512]{1,0:T(8,128)(2,1)}) custom-call(s32[4,32]{1,0:T(4,128)} %bitcast.12, bf16[256,256]{1,0:T(8,128)(2,1)} %bitcast.9, bf16[8,32]{1,0:T(8,128)(2,1)} %bitcast.13, s32[4,8,32]{2,1,0:T(8,128)} %bitcast.11, ...), custom_call_target="tpu_custom_call" | custom-call | tf_op jit(solution)/shard_map/exchange/pallas_call | solution.py:677
  30.9 33.9 %tile.1 = (bf16[1024,512]{1,0:T(8,128)(2,1)}, bf16[1024,512]{1,0:T(8,128)(2,1)}, bf16[2,1024,512]{2,1,0:T(8,128)(2,1)}, bf16[256,512]{1,0:T(8,128)(2,1)}, bf16[2...) custom-call(bf16[2048,256]{1,0:T(8,128)(2,1)} %bitcast.8, f32[128,128]{1,0:T(8,128)} %bitcast.10, ...), custom_call_target="tpu_custom_call" | custom-call | tf_op jit(solution)/shard_map/tile/pallas_call | solution.py:717
  64.8 39.6 %sum_grads.1 = (bf16[2,1024,512]{2,1,0:T(8,128)(2,1)}, bf16[2,128,512]{2,1,0:T(8,128)(2,1)}) custom-call(bf16[2,1024,512]{2,1,0:T(8,128)(2,1)} %get-tuple-element.29.main_ref, bf16[256,512]{1,0:T(8,128)(2,1)} %get-tuple-element.30.part_ref, bf16[2048,256]{1,0:T(8,128)(2,1)} %get-tuple-element.31.rows_ref, bf16[2048,512]{1,0:T(8,128)(2,1)} %get-tuple-element.32.slope_ref, ...), custom_call_target="tpu_custom_call" | custom-call | tf_op jit(solution)/shard_map/sum_grads/pallas_call | solution.py:647
  104.3 4.3 %widen.1 = (f32[256,512]{1,0:T(8,128)}, f32[512,1024]{1,0:T(8,128)}, f32[512,512]{1,0:T(8,128)}, f32[512,512]{1,0:T(8,128)}) custom-call(bf16[2,2,512,512]{3,2,1,0:T(8,128)(2,1)} %bitcast.7, bf16[2,128,512]{2,1,0:T(8,128)(2,1)} %get-tuple-element.35.gobs_ref), custom_call_target="tpu_custom_call" | custom-call | tf_op jit(solution)/shard_map/widen/pallas_call | solution.py:763

commit v4 on v3

v4 whole, which is shorter than its diff:
```python
import functools
import math

import jax
import jax.numpy as jnp
from jax import lax
from jax.experimental import pallas as pl
from jax.experimental.pallas import tpu as pltpu
from jax.sharding import PartitionSpec as P

HEADS = 8
GROUPS = 8
DEV = 128
OBS = 8
CAP = 2
CH = 256
D = 512
CELLS = 1024
GCELLS = CELLS // GROUPS
ROWS = DEV * CAP * OBS
KB = 128
MAXB = 24
LEAD = 18
SPAN = 768
F32 = jnp.float32
BF16 = jnp.bfloat16
NEG = -1e30
VMEM_LIMIT = 59 << 20
MESH = pl.DeviceIdType.MESH


def dot(a, b):
    return lax.dot_general(a, b, (((1,), (0,)), ((), ())), preferred_element_type=F32)


def dot_nt(a, b):
    return lax.dot_general(a, b, (((1,), (1,)), ((), ())), preferred_element_type=F32)


def dot_tn(a, b):
    return lax.dot_general(a, b, (((0,), (0,)), ((), ())), preferred_element_type=F32)


def iota(shape, dim):
    return lax.broadcasted_iota(jnp.int32, shape, dim)


def gelu_parts(x):
    a = jnp.abs(x)
    t = 1.0 / (1.0 + (0.3275911 / math.sqrt(2.0)) * a)
    e = jnp.exp(-0.5 * x * x)
    poly = t * (
        0.5 * 0.254829592
        + t * (-0.5 * 0.284496736 + t * (0.5 * 1.421413741 + t * (-0.5 * 1.453152027 + t * (0.5 * 1.061405429))))
    )
    tail = poly * e
    cdf = jnp.where(x < 0.0, tail, 1.0 - tail)
    return x * cdf, cdf + x * e * (1.0 / math.sqrt(2.0 * math.pi))


def hot(mask):
    return jnp.where(mask, 1.0, 0.0).astype(BF16)


def exchange_kernel(
    foot_ref, obs_ref, bias_ref, cell_ref, lat_ref, dout_ref, wq_ref, wo_ref,
    recv_ref, rmeta_ref, q_ref, back_ref,
    foot_v, obs_v, bias_v, cell_v, lat_v, dout_v, wq_v, wo_v, q_v, back_v,
    stage, mstage, osend, omsend, foot_s, marks_s, sem_in, sem_out, sem_core, sem_chip,
):
    lat, lon = lax.axis_index("lat"), lax.axis_index("lon")
    core = lax.rem(lat, 2)
    y, z, x = lat // 2, lon // 4, lax.rem(lon, 4)
    loads = []
    for i, (src, dst) in enumerate((
        (foot_ref, foot_v), (obs_ref, obs_v), (bias_ref, bias_v), (cell_ref, cell_v),
        (lat_ref, lat_v), (wq_ref, wq_v), (dout_ref, dout_v), (wo_ref, wo_v),
    )):
        loads.append(pltpu.make_async_copy(src, dst, sem_in.at[i]))
        loads[-1].start()

    ys = [lax.rem(y + d, 4) for d in range(4)]
    lons = [lax.rem(z + d // 4, 4) * 4 + lax.rem(x + d % 4, 4) for d in range(16)]
    chips = []
    for k in range(1, 64):
        cy, cl = ys[k // 16], lons[k % 16]
        chips.append((cy * 16 + cl, {"lat": cy * 2 + core, "lon": cl}))
    sibling = {"lat": y * 2 + 1 - core, "lon": lon}
    my_chip = y * 16 + lon
    barrier = pltpu.get_barrier_semaphore()
    pl.semaphore_signal(barrier, inc=1, device_id=sibling, device_id_type=MESH)
    for chip, where in chips:
        pl.semaphore_signal(barrier, inc=1, device_id=where, device_id_type=MESH)

    foot_s[...] = jnp.full((16, 128), -1.0, F32)
    marks_s[...] = jnp.zeros((128, 1280), F32)
    for load in loads[:4]:
        load.wait()
    foot_s[0:4, 0:32] = foot_v[...].astype(F32)
    for rank in range(CAP):
        lane, at = rank * OBS, rank * 640
        marks_s[lane : lane + OBS, at : at + 32] = bias_v[...].astype(F32)
        for f in range(4):
            lane, at = (CAP + rank) * OBS, rank * 640 + (1 + f) * 128
            marks_s[lane : lane + OBS, at : at + 32] = cell_v[f].astype(F32) - float(GROUPS)
    foot = foot_s[...]
    marks = marks_s[...].astype(BF16)
    r, c = iota((128, 128), 0), iota((128, 128), 1)
    upper = hot(r < c)
    widen = hot(iota((128, 256), 1) // OBS == iota((128, 256), 0))
    keep = iota((1024, 256), 0) % OBS == iota((1024, 256), 1) % OBS

    def slots_of(to_core):
        tile = (r // 32) * 32 + to_core * 16 + (r // CAP) % 16
        hit = jnp.zeros((128, 128), F32)
        for f in range(4):
            hit = hit + jnp.where(foot[f : f + 1, :] == tile.astype(F32), 1.0, 0.0)
        sel = hit * jnp.where(dot(hit.astype(BF16), upper) == (r % CAP).astype(F32), 1.0, 0.0)
        blocks = dot(sel.astype(BF16), widen)
        spread = jnp.broadcast_to(blocks[:, None, :], (128, OBS, 256)).reshape(1024, 256)
        rows = dot(jnp.where(keep, spread, 0.0).astype(BF16), obs_v[...]).astype(BF16)
        tile = iota((64, 128), 0)
        tile = ((tile // 16) * 32 + to_core * 16 + tile % 16).astype(F32)
        hits = [jnp.where(foot[f : f + 1, :] == tile, 1.0, 0.0) for f in range(4)]
        any_hit = hits[0] + hits[1] + hits[2] + hits[3]
        order = dot(any_hit.astype(BF16), upper)
        left = []
        for rank in range(CAP):
            chosen = any_hit * jnp.where(order == float(rank), 1.0, 0.0)
            left += [chosen] + [chosen * hits[f] for f in range(4)]
        meta = dot_nt(jnp.concatenate(left, axis=1).astype(BF16), marks)
        return rows.reshape(64, 16, CH), meta.reshape(64, 1, 128)

    osend[...], omsend[...] = slots_of(1 - core)
    pl.semaphore_wait(barrier, 64)

    def copy(src, dst, sems, where):
        return pltpu.make_async_remote_copy(
            src_ref=src, dst_ref=dst, send_sem=sems.at[0], recv_sem=sems.at[1], device_id=where, device_id_type=MESH,
        )

    swap = [copy(osend, stage.at[core], sem_core.at[0], sibling), copy(omsend, mstage.at[core], sem_core.at[1], sibling)]
    for part in swap:
        part.start()
    stage[core], mstage[core] = slots_of(core)
    for part in swap:
        part.wait_recv()
    for chip, where in chips:
        copy(stage.at[:, chip], recv_ref.at[:, my_chip], sem_chip.at[0], where).start()
        copy(mstage.at[:, chip], rmeta_ref.at[:, my_chip], sem_chip.at[1], where).start()
    stores = [
        pltpu.make_async_copy(stage.at[:, my_chip], recv_ref.at[:, my_chip], sem_out.at[0]),
        pltpu.make_async_copy(mstage.at[:, my_chip], rmeta_ref.at[:, my_chip], sem_out.at[1]),
    ]
    for store in stores:
        store.start()

    loads[4].wait()
    loads[5].wait()
    q_v[...] = (dot(lat_v[...], wq_v[...]).astype(BF16).astype(F32) * 0.125).astype(BF16)
    stores.append(pltpu.make_async_copy(q_v, q_ref, sem_out.at[2]))
    stores[-1].start()
    loads[6].wait()
    loads[7].wait()
    back_v[...] = dot_nt(dout_v[...], wo_v[...]).astype(BF16)
    stores.append(pltpu.make_async_copy(back_v, back_ref, sem_out.at[3]))
    stores[-1].start()

    whole = copy(stage.at[:, 0:63], recv_ref.at[:, 0:63], sem_chip.at[0], sibling)
    marks = copy(mstage.at[:, 0:63], rmeta_ref.at[:, 0:63], sem_chip.at[1], sibling)
    whole.wait_recv()
    marks.wait_recv()
    whole.wait_send()
    marks.wait_send()
    for part in swap:
        part.wait_send()
    for store in stores:
        store.wait()


def tile_kernel(
    recv_ref, rmeta_ref, q_ref, back_ref, lat_ref, dout_ref, wobs_ref, wkv_ref, wq_ref, wo_ref,
    upd_ref, dlat_ref, main_ref,
    rowst_s, slope_s, enct_s, kv_s, bias_s, attn_s, dq_s, dpre_s, sums_s, main_v, upd_v, dlat_v, meta_sm,
    recv_v, rmeta_v, q_s, back_s, lat_v, dout_v, wobs_v, wkv_v, wq_v, wo_v, sem_in, sem_out,
):
    loads = []
    for i, (src, dst) in enumerate((
        (rmeta_ref, rmeta_v), (recv_ref, recv_v), (wobs_ref, wobs_v), (wkv_ref, wkv_v), (q_ref, q_s), (back_ref, back_s),
        (lat_ref, lat_v), (dout_ref, dout_v), (wq_ref, wq_v), (wo_ref, wo_v),
    )):
        loads.append(pltpu.make_async_copy(src, dst, sem_in.at[i]))
        loads[-1].start()

    loads[0].wait()
    r, c = iota((128, 128), 0), iota((128, 128), 1)
    marks = rmeta_v[...].astype(BF16)
    own_lane = r % 8 == c // 16
    chunk = jnp.where(iota((16, 128), 0) == iota((16, 128), 1) // 8, 1.0, 0.0).astype(BF16)

    def laned(first_lane):
        lanes = dot(marks, jnp.where(r == c % 16 + first_lane, 1.0, 0.0).astype(BF16))
        return dot(chunk, jnp.where(own_lane, lanes, 0.0).astype(BF16))

    bias_row = laned(0)
    cell = laned(16) + float(GROUPS)
    inside = jnp.concatenate([jnp.where(cell == float(g), 1.0, 0.0) for g in range(GROUPS)], axis=0)
    upto = jnp.where(r <= c, 1.0, 0.0).astype(BF16)
    prefix = dot(inside.astype(BF16), upto)
    total = jnp.broadcast_to(prefix[:, 127:128], (128, 128)).astype(BF16)
    same = r // 16 == c // 16
    before = dot(jnp.where(same & (c < r), 1.0, 0.0).astype(BF16), total)
    count = dot(jnp.where(same, 1.0, 0.0).astype(BF16), total)
    nblk = jnp.floor((count + (KB - 1.0)) * (1.0 / KB))
    first = dot(jnp.where((c % 16 == 0) & (c // 16 < r // 16), 1.0, 0.0).astype(BF16), nblk.astype(BF16))
    place = jnp.where(inside > 0.5, first * float(KB) + before + prefix - 1.0, -1.0)
    pos = place[0:16, :]
    for g in range(1, GROUPS):
        pos = jnp.maximum(pos, place[g * 16 : (g + 1) * 16, :])
    for g in range(GROUPS):
        meta_sm[0, g] = jnp.max(first[g * 16 : g * 16 + 8, :]).astype(jnp.int32)
        meta_sm[1, g] = jnp.max(nblk[g * 16 : g * 16 + 8, :]).astype(jnp.int32)
        meta_sm[2, g] = jnp.max(count[g * 16 : g * 16 + 8, :]).astype(jnp.int32)
    blocks = meta_sm[0, GROUPS - 1] + meta_sm[1, GROUPS - 1]

    lane_pos = [jnp.broadcast_to(pos[i : i + 1, :], (16, 128)) for i in range(16)]
    lane_bias = [jnp.broadcast_to(bias_row[i : i + 1, :], (16, 128)).astype(BF16) for i in range(16)]
    row_id = iota((256, 128), 0).astype(F32).astype(BF16)

    def gather(base, rows):
        cols = []
        bias = jnp.zeros((rows, 128), BF16)
        for i in range(16):
            rel = jnp.clip(lane_pos[i] - base, -1.0, float(rows)).astype(BF16)
            found = row_id[0:rows] == jnp.concatenate([rel] * (rows // 16), axis=0)
            cols.append(jnp.where(found, jnp.ones((), BF16), jnp.zeros((), BF16)))
            bias = jnp.where(found, jnp.concatenate([lane_bias[i]] * (rows // 16), axis=0), bias)
        bias = jnp.sum(bias.astype(F32), axis=1, keepdims=True)
        return jnp.concatenate(cols, axis=1), jnp.broadcast_to(bias, (rows, 128))

    def picked(at, picks):
        bias_s[at, :] = jnp.concatenate([pick[1] for pick in picks], axis=0)
        rows = dot(jnp.concatenate([pick[0] for pick in picks], axis=0), recv_v[...]).astype(BF16)
        rowst_s[:, at] = rows.T
        return dot(rows, wobs_v[...])

    def encoded(at, pre):
        value, slope = gelu_parts(pre)
        enc = value.astype(BF16)
        slope_s[at, :] = slope
        enct_s[:, at] = enc.T
        kv_s[at, :] = dot(enc, wkv_v[...]).astype(BF16)

    for load in loads[1:4]:
        load.wait()
    last = None
    for i in range(LEAD * KB // SPAN):
        at = slice(i * SPAN, (i + 1) * SPAN)
        pre = picked(at, [gather(float(i * SPAN + j), 256) for j in range(0, SPAN, 256)])
        if last is not None:
            encoded(*last)
        last = (at, pre)
    encoded(*last)

    def encode(b, carry):
        at = pl.ds(pl.multiple_of(b * KB, KB), KB)
        encoded(at, picked(at, [gather((b * KB).astype(F32), KB)]))
        return carry

    lax.fori_loop(LEAD, blocks, encode, 0)
    for load in loads[4:6]:
        load.wait()

    lane_head = iota((GCELLS, 256), 1) // 64

    def spread_heads(x):
        return jnp.concatenate([jnp.where(lane_head == h, x, jnp.zeros((), BF16)) for h in range(4)], axis=0)

    def scores(r0, rows, valid, half, qq):
        keys = kv_s[pl.ds(r0, rows), half * 256 : half * 256 + 256]
        bias = jnp.where(iota((rows, 128), 0) < valid, bias_s[pl.ds(r0, rows), :], NEG)
        return dot_nt(keys, qq) + jnp.concatenate([bias] * 4, axis=1)

    def dprobs(r0, rows, half, bb):
        return dot_nt(kv_s[pl.ds(r0, rows), D + half * 256 : D + half * 256 + 256], bb)

    def diagonal(x):
        out = x[0:GCELLS]
        for h in range(1, 4):
            out = jnp.where(lane_head == h, x[h * GCELLS : (h + 1) * GCELLS], out)
        return out

    def products(r0, rows, half, wb, ds, qq, bb):
        keys = kv_s[pl.ds(r0, rows), half * 256 : half * 256 + 256]
        values = kv_s[pl.ds(r0, rows), D + half * 256 : D + half * 256 + 256]
        attn = diagonal(dot(wb.T, values))
        dq = diagonal(dot(ds.T, keys))
        return attn, dq, dot(ds, qq).astype(BF16), dot(wb, bb).astype(BF16)

    def put_keys(r0, rows, half, dk, dv):
        kv_s[pl.ds(r0, rows), half * 256 : half * 256 + 256] = dk
        kv_s[pl.ds(r0, rows), D + half * 256 : D + half * 256 + 256] = dv

    def heads(c0, half):
        lanes = slice(half * 256, half * 256 + 256)
        return spread_heads(q_s[pl.ds(c0, GCELLS), lanes]), spread_heads(back_s[pl.ds(c0, GCELLS), lanes])

    def put(c0, half, attn, dq):
        lanes = slice(half * 256, half * 256 + 256)
        attn_s[pl.ds(c0, GCELLS), lanes] = attn.astype(BF16)
        dq_s[pl.ds(c0, GCELLS), lanes] = (dq * 0.125).astype(BF16)

    def at_once(groups, rows):
        jobs = []
        for g in groups:
            r0, c0 = pl.multiple_of(meta_sm[0, g] * KB, KB), pl.multiple_of(g * GCELLS, GCELLS)
            for half in range(2):
                jobs.append((r0, c0, half, meta_sm[2, g]) + heads(c0, half))
        raw = [scores(r0, rows, valid, half, qq) for r0, _, half, valid, qq, _ in jobs]
        dps = [dprobs(r0, rows, half, bb) for r0, _, half, _, _, bb in jobs]
        done = []
        for (r0, _, half, _, qq, bb), s, dp in zip(jobs, raw, dps):
            top = jnp.maximum(jnp.max(s, axis=0, keepdims=True), 0.0)
            p = jnp.exp(s - top)
            inv = 1.0 / (jnp.exp(-top) + jnp.sum(p, axis=0, keepdims=True))
            weights = p * inv
            delta = jnp.sum(weights * dp, axis=0, keepdims=True)
            wb, ds = weights.astype(BF16), (weights * (dp - delta)).astype(BF16)
            done.append(products(r0, rows, half, wb, ds, qq, bb))
        for (r0, c0, half, _, _, _), (attn, dq, dk, dv) in zip(jobs, done):
            put_keys(r0, rows, half, dk, dv)
            put(c0, half, attn, dq)

    def by_chunks(g):
        start, nb, count = meta_sm[0, g], meta_sm[1, g], meta_sm[2, g]
        c0 = pl.multiple_of(g * GCELLS, GCELLS)
        for half in range(2):
            qq, bb = heads(c0, half)

            def row(b):
                return pl.multiple_of((start + b) * KB, KB)

            def score(b):
                return scores(row(b), KB, count - b * KB, half, qq)

            def first_pass(b, top):
                return jnp.maximum(top, jnp.max(score(b), axis=0, keepdims=True))

            top = lax.fori_loop(0, nb, first_pass, jnp.zeros((1, 512), F32))

            def second_pass(b, sums):
                p = jnp.exp(score(b) - top)
                dp = dprobs(row(b), KB, half, bb)
                return (
                    sums[0] + jnp.sum(p, axis=0, keepdims=True),
                    sums[1] + jnp.sum(p * dp, axis=0, keepdims=True),
                )

            sums = lax.fori_loop(0, nb, second_pass, (jnp.exp(-top), jnp.zeros((1, 512), F32)))
            inv = 1.0 / sums[0]
            delta = sums[1] * inv

            def third_pass(b, acc):
                weights = jnp.exp(score(b) - top) * inv
                dp = dprobs(row(b), KB, half, bb)
                wb, ds = weights.astype(BF16), (weights * (dp - delta)).astype(BF16)
                attn, dq, dk, dv = products(row(b), KB, half, wb, ds, qq, bb)
                put_keys(row(b), KB, half, dk, dv)
                return acc[0] + attn, acc[1] + dq

            zero = jnp.zeros((GCELLS, 256), F32)
            put(c0, half, *lax.fori_loop(0, nb, third_pass, (zero, zero)))

    def single(g):
        nb = meta_sm[1, g]
        for size in (1, 2, 3):

            @pl.when(nb == size)
            def _():
                at_once((g,), size * KB)

        @pl.when((nb < 1) | (nb > 3))
        def _():
            by_chunks(g)

    def pair(i, carry):
        one, two = 2 * i, 2 * i + 1
        alike = (meta_sm[1, one] == 2) & (meta_sm[1, two] == 2)

        @pl.when(alike)
        def _():
            at_once((one, two), 2 * KB)

        @pl.when(jnp.logical_not(alike))
        def _():
            lax.fori_loop(one, two + 1, lambda g, c: (single(g), c)[1], 0)

        return carry

    lax.fori_loop(0, GROUPS // 2, pair, 0)

    for load in loads[6:]:
        load.wait()
    attn, dq = attn_s[...], dq_s[...]
    outs = []

    def put_out(src, dst):
        outs.append(pltpu.make_async_copy(src, dst, sem_out.at[len(outs)]))
        outs[-1].start()

    upd_v[...] = (lat_v[...].astype(F32) + dot(attn, wo_v[...])).astype(BF16)
    put_out(upd_v, upd_ref)
    dlat_v[...] = (dout_v[...].astype(F32) + dot_nt(dq, wq_v[...])).astype(BF16)
    put_out(dlat_v, dlat_ref)
    main_v[0, 0:512, :] = dot_tn(lat_v[...], dq).astype(BF16)
    main_v[1, 0:512, :] = dot_tn(attn, dout_v[...]).astype(BF16)

    def through_encoder(at):
        return (dot_nt(kv_s[at, :], wkv_v[...]) * slope_s[at, :]).astype(BF16)

    lead = LEAD * KB
    for i in range(lead // SPAN):
        dpre_s[i * SPAN : (i + 1) * SPAN, :] = through_encoder(slice(i * SPAN, (i + 1) * SPAN))

    def lead_kv(i):
        return dot(enct_s[:, 0:lead], kv_s[0:lead, i * 256 : (i + 1) * 256])

    lead_obs = dot(rowst_s[:, 0:lead], dpre_s[...])

    @pl.when(blocks <= LEAD)
    def _():
        for i in range(4):
            main_v[i // 2, 512:1024, i % 2 * 256 : i % 2 * 256 + 256] = lead_kv(i).astype(BF16)
        for h in range(2):
            main_v[h, 1024:1152, :] = lead_obs[h * 128 : (h + 1) * 128].astype(BF16)

    @pl.when(blocks > LEAD)
    def _():
        for i in range(4):
            sums_s[0:512, i * 256 : (i + 1) * 256] = lead_kv(i)
        sums_s[512:768, 0:512] = lead_obs

        def encoder_grads(b, carry):
            at = pl.ds(pl.multiple_of(b * KB, KB), KB)
            sums_s[0:512, :] += dot(enct_s[:, at], kv_s[at, :])
            sums_s[512:768, 0:512] += dot(rowst_s[:, at], through_encoder(at))
            return carry

        lax.fori_loop(LEAD, blocks, encoder_grads, 0)
        for h in range(2):
            main_v[h, 512:1024, :] = sums_s[0:512, h * 512 : (h + 1) * 512].astype(BF16)
            main_v[h, 1024:1152, :] = sums_s[512 + h * 128 : 640 + h * 128, 0:512].astype(BF16)

    put_out(main_v, main_ref)
    for out in outs:
        out.wait()


ORDER = ("x", "y", "z")
JOBS = ((0, 384, 0), (384, 384, 1), (768, 384, 2))
HALF = 1152


def peer(step_axis, k):
    lat, lon = lax.axis_index("lat"), lax.axis_index("lon")
    y, core, z, x = lat // 2, lat % 2, lon // 4, lon % 4
    if step_axis == "x":
        x = (x + k) % 4
    elif step_axis == "y":
        y = (y + k) % 4
    elif step_axis == "z":
        z = (z + k) % 4
    else:
        core = 1 - core
    return {"lat": y * 2 + core, "lon": z * 4 + x}


def place_on(step_axis):
    lat, lon = lax.axis_index("lat"), lax.axis_index("lon")
    return {"x": lon % 4, "y": lat // 2, "z": lon // 4}[step_axis]


class Job:
    def __init__(self, far, near, out, half, start, rows, turn, bufs, sems):
        self.far, self.near, self.start, self.rows, self.piece = far, near, start, rows, rows // 4
        self.axes = [ORDER[(turn + i) % 3] for i in range(3)]
        self.core_recv, self.src1, self.recv1, self.src2, self.recv2, self.buf3 = bufs
        self.sems, self.half, self.phase, self.sent = sems, half, -1, []
        self.result = out.at[half, pl.ds(start, rows), :]

    def describe(self, src, dst, axis, k):
        return pltpu.make_async_remote_copy(
            src_ref=src, dst_ref=dst, send_sem=self.sems.at[self.phase, 0], recv_sem=self.sems.at[self.phase, 1],
            device_id=peer(axis, k), device_id_type=MESH,
        )

    def across(self, src, dst):
        self.phase += 1
        copy = self.describe(src, dst, "core", 1)
        copy.start()
        self.sent.append(copy)

    def around(self, axis, src_of, dst_of, whole):
        self.phase += 1
        for k in range(1, 4):
            self.describe(src_of(k), dst_of(k), axis, k).start()
        self.sent.append(self.describe(whole, whole, axis, 1))

    def arrived(self):
        self.sent[-1].wait_recv()

    def swap(self):
        self.across(self.far.at[1 - self.half, pl.ds(self.start, self.rows), :], self.core_recv)

    def scatter1(self):
        self.arrived()
        own = self.near[self.half, self.start : self.start + self.rows, :].astype(F32)
        total = (own + self.core_recv[...].astype(F32)).astype(BF16)
        for j in range(4):
            self.src1[j] = total[j * self.piece : (j + 1) * self.piece, :]
        at = place_on(self.axes[0])
        self.around(
            self.axes[0], lambda k: self.src1.at[lax.rem(at + k, 4)], lambda k: self.recv1.at[k - 1], self.recv1
        )

    def scatter2(self):
        self.arrived()
        total = self.src1[place_on(self.axes[0])].astype(F32)
        for k in range(3):
            total = total + self.recv1[k].astype(F32)
        for j in range(4):
            self.src2[j] = total[:, j * 128 : (j + 1) * 128].astype(BF16)
        at = place_on(self.axes[1])
        self.around(
            self.axes[1], lambda k: self.src2.at[lax.rem(at + k, 4)], lambda k: self.recv2.at[k - 1], self.recv2
        )

    def exchange3(self):
        self.arrived()
        total = self.src2[place_on(self.axes[1])].astype(F32)
        for k in range(3):
            total = total + self.recv2[k].astype(F32)
        self.buf3[0] = total.astype(BF16)
        self.around(self.axes[2], lambda k: self.buf3.at[0], lambda k: self.buf3.at[k], self.buf3.at[1:4])

    def gather2(self):
        self.arrived()
        at = place_on(self.axes[2])
        total = self.buf3[at].astype(F32)
        for s in range(1, 4):
            total = total + self.buf3[lax.rem(at + 4 - s, 4)].astype(F32)
        rows = pl.ds(pl.multiple_of(place_on(self.axes[0]) * self.piece, self.piece), self.piece)
        lanes = pl.ds(pl.multiple_of(place_on(self.axes[1]) * 128, 128), 128)
        self.result[rows, lanes] = total.astype(BF16)
        mine = self.result.at[rows, lanes]
        self.around(self.axes[1], lambda k: mine, lambda k: mine, self.recv2)

    def gather1(self):
        self.arrived()
        mine = self.result.at[pl.ds(pl.multiple_of(place_on(self.axes[0]) * self.piece, self.piece), self.piece), :]
        self.around(self.axes[0], lambda k: mine, lambda k: mine, self.recv1)

    def share(self):
        self.arrived()
        self.across(self.result, self.result)

    def settle(self):
        for copy in self.sent:
            copy.wait_send()


def sum_kernel(main_ref, out_ref, main_v, out_v, sem_in, sem_out, *scratch):
    half = lax.rem(lax.axis_index("lat"), 2)
    load = pltpu.make_async_copy(main_ref.at[half], main_v.at[half], sem_in)
    load.start()
    barrier = pltpu.get_barrier_semaphore()
    pl.semaphore_signal(barrier, inc=1, device_id=peer("core", 1), device_id_type=MESH)
    for axis in ORDER:
        for k in range(1, 4):
            pl.semaphore_signal(barrier, inc=1, device_id=peer(axis, k), device_id_type=MESH)
    jobs = []
    for i, (start, rows, turn) in enumerate(JOBS):
        jobs.append(Job(main_ref, main_v, out_v, half, start, rows, turn, scratch[7 * i : 7 * i + 6], scratch[7 * i + 6]))
    stores = []

    def store(job, i, h):
        at = pl.ds(job.start, job.rows)
        stores.append(pltpu.make_async_copy(out_v.at[h, at, :], out_ref.at[h, at, :], sem_out.at[i]))
        stores[-1].start()

    pl.semaphore_wait(barrier, 10)
    for job in jobs:
        job.swap()
    load.wait()
    for what in ("scatter1", "scatter2", "exchange3", "gather2", "gather1"):
        for job in jobs:
            getattr(job, what)()
    for i, job in enumerate(jobs):
        job.share()
        store(job, i, half)
    for i, job in enumerate(jobs):
        job.arrived()
        store(job, 3 + i, 1 - half)
    for job in jobs:
        job.settle()
    for copy in stores:
        copy.wait()


def widen_kernel(gobs_ref, gkv_ref, gqo_ref, obs_ref, kv_ref, q_ref, o_ref):
    obs_ref[...] = gobs_ref[0].astype(F32)
    q_ref[...] = gqo_ref[0].astype(F32)
    o_ref[...] = gqo_ref[1].astype(F32)
    for h in range(2):
        kv_ref[:, h * D : (h + 1) * D] = gkv_ref[h].astype(F32)


def sum_grads(main):
    far = pl.BlockSpec(memory_space=pltpu.HBM)
    dma = pltpu.SemaphoreType.DMA
    scratch = []
    for _, n, _ in JOBS:
        piece = n // 4
        scratch += [
            pltpu.VMEM((n, D), BF16),
            pltpu.VMEM((4, piece, D), BF16),
            pltpu.VMEM((3, piece, D), BF16),
            pltpu.VMEM((4, piece, 128), BF16),
            pltpu.VMEM((3, piece, 128), BF16),
            pltpu.VMEM((4, piece, 128), BF16),
            dma((7, 2)),
        ]
    return pl.pallas_call(
        sum_kernel,
        out_shape=jax.ShapeDtypeStruct((2, HALF, D), BF16),
        in_specs=[far],
        out_specs=far,
        scratch_shapes=[
            pltpu.VMEM((2, HALF, D), BF16),
            pltpu.VMEM((2, HALF, D), BF16),
            dma,
            dma((6,)),
        ] + scratch,
        compiler_params=pltpu.CompilerParams(
            collective_id=1, has_side_effects=True, vmem_limit_bytes=VMEM_LIMIT
        ),
        name="sum_grads",
    )(main)


def body(latents, d_out, observations, obs_bias, footprint, obs_cell, w_obs, w_kv, w_q, w_o):
    vmem = pl.BlockSpec(memory_space=pltpu.VMEM)
    dma = pltpu.SemaphoreType.DMA
    far = pl.BlockSpec(memory_space=pltpu.HBM)
    recv, rmeta, q, back = pl.pallas_call(
        exchange_kernel,
        out_shape=(
            jax.ShapeDtypeStruct((2, 64, 16, CH), BF16),
            jax.ShapeDtypeStruct((2, 64, 1, 128), F32),
            jax.ShapeDtypeStruct((CELLS, D), BF16),
            jax.ShapeDtypeStruct((CELLS, D), BF16),
        ),
        in_specs=[far] * 8,
        out_specs=[far] * 4,
        scratch_shapes=[
            pltpu.VMEM((4, 32), jnp.int32),
            pltpu.VMEM((32 * OBS, CH), BF16),
            pltpu.VMEM((OBS, 32), BF16),
            pltpu.VMEM((4, OBS, 32), jnp.int32),
            pltpu.VMEM((CELLS, D), BF16),
            pltpu.VMEM((CELLS, D), BF16),
            pltpu.VMEM((D, D), BF16),
            pltpu.VMEM((D, D), BF16),
            pltpu.VMEM((CELLS, D), BF16),
            pltpu.VMEM((CELLS, D), BF16),
            pltpu.VMEM((2, 64, 16, CH), BF16),
            pltpu.VMEM((2, 64, 1, 128), F32),
            pltpu.VMEM((64, 16, CH), BF16),
            pltpu.VMEM((64, 1, 128), F32),
            pltpu.VMEM((16, 128), F32),
            pltpu.VMEM((128, 1280), F32),
            dma((8,)),
            dma((4,)),
            dma((2, 2)),
            dma((2, 2)),
        ],
        compiler_params=pltpu.CompilerParams(
            collective_id=0, has_side_effects=True, vmem_limit_bytes=VMEM_LIMIT
        ),
        name="exchange",
    )(
        footprint.T, observations.reshape(-1, CH), obs_bias.T, obs_cell.transpose(1, 2, 0),
        latents, d_out, w_q, w_o,
    )
    upd, dlat, main = pl.pallas_call(
        tile_kernel,
        out_shape=(
            jax.ShapeDtypeStruct((CELLS, D), BF16),
            jax.ShapeDtypeStruct((CELLS, D), BF16),
            jax.ShapeDtypeStruct((2, HALF, D), BF16),
        ),
        in_specs=[far] * 10,
        out_specs=[far] * 3,
        scratch_shapes=[
            pltpu.VMEM((CH, MAXB * KB), BF16),
            pltpu.VMEM((MAXB * KB, D), F32),
            pltpu.VMEM((D, MAXB * KB), BF16),
            pltpu.VMEM((MAXB * KB, 2 * D), BF16),
            pltpu.VMEM((MAXB * KB, 128), F32),
            pltpu.VMEM((CELLS, D), BF16),
            pltpu.VMEM((CELLS, D), BF16),
            pltpu.VMEM((LEAD * KB, D), BF16),
            pltpu.VMEM((768, 2 * D), F32),
            pltpu.VMEM((2, HALF, D), BF16),
            pltpu.VMEM((CELLS, D), BF16),
            pltpu.VMEM((CELLS, D), BF16),
            pltpu.SMEM((3, GROUPS), jnp.int32),
            pltpu.VMEM((ROWS, CH), BF16),
            pltpu.VMEM((DEV, 128), F32),
            pltpu.VMEM((CELLS, D), BF16),
            pltpu.VMEM((CELLS, D), BF16),
            pltpu.VMEM((CELLS, D), BF16),
            pltpu.VMEM((CELLS, D), BF16),
            pltpu.VMEM((CH, D), BF16),
            pltpu.VMEM((D, 2 * D), BF16),
            pltpu.VMEM((D, D), BF16),
            pltpu.VMEM((D, D), BF16),
            dma((10,)),
            dma((3,)),
        ],
        compiler_params=pltpu.CompilerParams(vmem_limit_bytes=VMEM_LIMIT),
        name="tile",
    )(recv.reshape(ROWS, CH), rmeta.reshape(DEV, 128), q, back, latents, d_out, w_obs, w_kv, w_q, w_o)
    total = sum_grads(main)
    gobs, gkv, gq, go = pl.pallas_call(
        widen_kernel,
        grid=(4,),
        out_shape=[jax.ShapeDtypeStruct(x.shape, F32) for x in (w_obs, w_kv, w_q, w_o)],
        in_specs=[
            pl.BlockSpec((1, 64, D), lambda i: (i // 2, 16 + i % 2, 0)),
            pl.BlockSpec((2, 128, D), lambda i: (0, 4 + i, 0)),
            pl.BlockSpec((2, 128, D), lambda i: (0, i, 0)),
        ],
        out_specs=[
            pl.BlockSpec((64, D), lambda i: (i, 0)),
            pl.BlockSpec((128, 2 * D), lambda i: (i, 0)),
            pl.BlockSpec((128, D), lambda i: (i, 0)),
            pl.BlockSpec((128, D), lambda i: (i, 0)),
        ],
        compiler_params=pltpu.CompilerParams(vmem_limit_bytes=VMEM_LIMIT),
        name="widen",
    )(total, total, total)
    return upd, dlat, gobs, gkv, gq, go


def solution(mesh):
    spread = ("lat", "lon")
    placed = (
        P(spread, None), P(spread, None), P(spread, None, None), P(spread, None), P(spread, None),
        P(spread, None, None), P(), P(), P(), P(),
    )
    return jax.shard_map(
        body,
        mesh=mesh,
        in_specs=placed,
        out_specs=(P(spread, None), P(spread, None), P(), P(), P(), P()),
        check_vma=False,
    )
```

time: 109 us -> 102 us (0.936)
  Pallas kernels: 108 us -> 101 us
    pallas_call x1, Pallas kernels: 39.6 us -> 34.5 us  [sum_grads(): pl.pallas_call(sum_kernel, out_shape=jax.ShapeDtypeStruct((2, HALF, D), B...]
    pallas_call x1, Pallas kernels: 33.9 us -> 32.3 us  [body(): pl.pallas_call(tile_kernel, out_shape=(jax.ShapeDtypeStruct((CELLS, D), B...]
where the time goes in v4:
time: 102 us
  Pallas kernels  101 us (99%)
    pallas_call x1, Pallas kernels, sum_grads(): pl.pallas_call(sum_kernel, out_shape=jax.ShapeDtypeStruct((2, HALF, D), B...  34.5 us
    pallas_call x1, Pallas kernels, body(): pl.pallas_call(tile_kernel, out_shape=(jax.ShapeDtypeStruct((CELLS, D), B...  32.3 us
    pallas_call x1, Pallas kernels, body(): pl.pallas_call(exchange_kernel, out_shape=(jax.ShapeDtypeStruct((2, 64, 1...  30.3 us
    pallas_call x1, Pallas kernels, body(): pl.pallas_call(widen_kernel, grid=(4,), out_shape=[jax.ShapeDtypeStruct(x...  4.33 us

profile of v4, /device:TPU:1, one launch (start us, length us, event | category | flops | bytes accessed | tf_op | source)
XLA Modules:
  0.0 102.1 jit_solution(3268313024630626666)
XLA Ops:
  0.6 30.3 %exchange.1 = (bf16[2,64,16,256]{3,2,1,0:T(8,128)(2,1)}, f32[2,64,1,128]{3,2,1,0:T(1,128)}, bf16[1024,512]{1,0:T(8,128)(2,1)}, bf16[1024,512]{1,0:T(8,128)(2,1)}) custom-call(s32[4,32]{1,0:T(4,128)} %bitcast.10, bf16[256,256]{1,0:T(8,128)(2,1)} %bitcast.7, bf16[8,32]{1,0:T(8,128)(2,1)} %bitcast.11, s32[4,8,32]{2,1,0:T(8,128)} %bitcast.9, ...), custom_call_target="tpu_custom_call" | custom-call | tf_op jit(solution)/shard_map/exchange/pallas_call | solution.py:655
  30.9 32.3 %tile.1 = (bf16[1024,512]{1,0:T(8,128)(2,1)}, bf16[1024,512]{1,0:T(8,128)(2,1)}, bf16[2,1152,512]{2,1,0:T(8,128)(2,1)}) custom-call(bf16[2048,256]{1,0:T(8,128)(2,1)} %bitcast.6, f32[128,128]{1,0:T(8,128)} %bitcast.8, bf16[1024,512]{1,0:T(8,128)(2,1)} %get-tuple-element.19.q_ref, bf16[1024,512]{1,0:T(8,128)(2,1)} %get-tuple-element.20.back_ref, ...), custom_call_target="tpu_custom_call" | custom-call | tf_op jit(solution)/shard_map/tile/pallas_call | solution.py:695
  63.3 34.5 %sum_grads.1.gobs_ref.gkv_ref.gqo_ref = bf16[2,1152,512]{2,1,0:T(8,128)(2,1)} custom-call(bf16[2,1152,512]{2,1,0:T(8,128)(2,1)} %get-tuple-element.23.main_ref), custom_call_target="tpu_custom_call" | custom-call | tf_op jit(solution)/shard_map/sum_grads/pallas_call | solution.py:633
  97.8 4.3 %widen.1 = (f32[256,512]{1,0:T(8,128)}, f32[512,1024]{1,0:T(8,128)}, f32[512,512]{1,0:T(8,128)}, f32[512,512]{1,0:T(8,128)}) custom-call(bf16[2,1152,512]{2,1,0:T(8,128)(2,1)} %sum_grads.1.gobs_ref.gkv_ref.gqo_ref, bf16[2,1152,512]{2,1,0:T(8,128)(2,1)} %sum_grads.1.gobs_ref.gkv_ref.gqo_ref, bf16[2,1152,512]{2,1,0:T(8,128)(2,1)} %sum_grads.1.gobs_ref.gkv_ref.gqo_ref), custom_call_target="tpu_custom_call" | custom-call | tf_op jit(solution)/shard_map/widen/pallas_call | solution.py:735

commit v5 on v4

--- a/solution.py
+++ b/solution.py
@@ -132,6 +132,7 @@
         return rows.reshape(64, 16, CH), meta.reshape(64, 1, 128)
 
     osend[...], omsend[...] = slots_of(1 - core)
+    stage[core], mstage[core] = slots_of(core)
     pl.semaphore_wait(barrier, 64)
 
     def copy(src, dst, sems, where):
@@ -142,12 +143,13 @@
     swap = [copy(osend, stage.at[core], sem_core.at[0], sibling), copy(omsend, mstage.at[core], sem_core.at[1], sibling)]
     for part in swap:
         part.start()
-    stage[core], mstage[core] = slots_of(core)
+    for chip, where in chips:
+        copy(stage.at[core, chip], recv_ref.at[core, my_chip], sem_chip.at[0], where).start()
     for part in swap:
         part.wait_recv()
     for chip, where in chips:
-        copy(stage.at[:, chip], recv_ref.at[:, my_chip], sem_chip.at[0], where).start()
-        copy(mstage.at[:, chip], rmeta_ref.at[:, my_chip], sem_chip.at[1], where).start()
+        copy(stage.at[1 - core, chip], recv_ref.at[1 - core, my_chip], sem_chip.at[1], where).start()
+        copy(mstage.at[:, chip], rmeta_ref.at[:, my_chip], sem_chip.at[2], where).start()
     stores = [
         pltpu.make_async_copy(stage.at[:, my_chip], recv_ref.at[:, my_chip], sem_out.at[0]),
         pltpu.make_async_copy(mstage.at[:, my_chip], rmeta_ref.at[:, my_chip], sem_out.at[1]),
@@ -166,12 +168,15 @@
     stores.append(pltpu.make_async_copy(back_v, back_ref, sem_out.at[3]))
     stores[-1].start()
 
-    whole = copy(stage.at[:, 0:63], recv_ref.at[:, 0:63], sem_chip.at[0], sibling)
-    marks = copy(mstage.at[:, 0:63], rmeta_ref.at[:, 0:63], sem_chip.at[1], sibling)
-    whole.wait_recv()
-    marks.wait_recv()
-    whole.wait_send()
-    marks.wait_send()
+    whole = [
+        copy(stage.at[core, 0:63], recv_ref.at[core, 0:63], sem_chip.at[0], sibling),
+        copy(stage.at[1 - core, 0:63], recv_ref.at[1 - core, 0:63], sem_chip.at[1], sibling),
+        copy(mstage.at[:, 0:63], rmeta_ref.at[:, 0:63], sem_chip.at[2], sibling),
+    ]
+    for part in whole:
+        part.wait_recv()
+    for part in whole:
+        part.wait_send()
     for part in swap:
         part.wait_send()
     for store in stores:
@@ -457,7 +462,7 @@
 
 
 ORDER = ("x", "y", "z")
-JOBS = ((0, 384, 0), (384, 384, 1), (768, 384, 2))
+JOBS = tuple((i * 128, 128, i % 3) for i in range(9))
 HALF = 1152
 
 
@@ -600,7 +605,7 @@
         store(job, i, half)
     for i, job in enumerate(jobs):
         job.arrived()
-        store(job, 3 + i, 1 - half)
+        store(job, len(JOBS) + i, 1 - half)
     for job in jobs:
         job.settle()
     for copy in stores:
@@ -639,7 +644,7 @@
             pltpu.VMEM((2, HALF, D), BF16),
             pltpu.VMEM((2, HALF, D), BF16),
             dma,
-            dma((6,)),
+            dma((2 * len(JOBS),)),
         ] + scratch,
         compiler_params=pltpu.CompilerParams(
             collective_id=1, has_side_effects=True, vmem_limit_bytes=VMEM_LIMIT
@@ -682,7 +687,7 @@
             dma((8,)),
             dma((4,)),
             dma((2, 2)),
-            dma((2, 2)),
+            dma((3, 2)),
         ],
         compiler_params=pltpu.CompilerParams(
             collective_id=0, has_side_effects=True, vmem_limit_bytes=VMEM_LIMIT

time: 102 us -> 93.9 us (0.921)
  Pallas kernels: 101 us -> 93 us
    pallas_call x1, Pallas kernels: 30.3 us -> 24.2 us  [body(): pl.pallas_call(exchange_kernel, out_shape=(jax.ShapeDtypeStruct((2, 64, 1...]
    pallas_call x1, Pallas kernels: 34.5 us -> 32.2 us  [sum_grads(): pl.pallas_call(sum_kernel, out_shape=jax.ShapeDtypeStruct((2, HALF, D), B...]
where the time goes in v5:
time: 93.9 us; the launch traced here: 93.7 us
  Pallas kernels  93 us (99%)
    pallas_call x1, Pallas kernels, body(): pl.pallas_call(tile_kernel, out_shape=(jax.ShapeDtypeStruct((CELLS, D), B...  32.3 us
    pallas_call x1, Pallas kernels, sum_grads(): pl.pallas_call(sum_kernel, out_shape=jax.ShapeDtypeStruct((2, HALF, D), B...  32.2 us
    pallas_call x1, Pallas kernels, body(): pl.pallas_call(exchange_kernel, out_shape=(jax.ShapeDtypeStruct((2, 64, 1...  24.2 us
    pallas_call x1, Pallas kernels, body(): pl.pallas_call(widen_kernel, grid=(4,), out_shape=[jax.ShapeDtypeStruct(x...  4.33 us

profile of v5, /device:TPU:1, one launch (start us, length us, event | category | flops | bytes accessed | tf_op | source)
XLA Modules:
  0.0 93.7 jit_solution(9748570537818010910)
XLA Ops:
  0.6 24.2 %exchange.1 = (bf16[2,64,16,256]{3,2,1,0:T(8,128)(2,1)}, f32[2,64,1,128]{3,2,1,0:T(1,128)}, bf16[1024,512]{1,0:T(8,128)(2,1)}, bf16[1024,512]{1,0:T(8,128)(2,1)}) custom-call(s32[4,32]{1,0:T(4,128)} %bitcast.10, bf16[256,256]{1,0:T(8,128)(2,1)} %bitcast.7, bf16[8,32]{1,0:T(8,128)(2,1)} %bitcast.11, s32[4,8,32]{2,1,0:T(8,128)} %bitcast.9, ...), custom_call_target="tpu_custom_call" | custom-call | tf_op jit(solution)/shard_map/exchange/pallas_call | solution.py:660
  24.9 32.3 %tile.1 = (bf16[1024,512]{1,0:T(8,128)(2,1)}, bf16[1024,512]{1,0:T(8,128)(2,1)}, bf16[2,1152,512]{2,1,0:T(8,128)(2,1)}) custom-call(bf16[2048,256]{1,0:T(8,128)(2,1)} %bitcast.6, f32[128,128]{1,0:T(8,128)} %bitcast.8, bf16[1024,512]{1,0:T(8,128)(2,1)} %get-tuple-element.19.q_ref, bf16[1024,512]{1,0:T(8,128)(2,1)} %get-tuple-element.20.back_ref, ...), custom_call_target="tpu_custom_call" | custom-call | tf_op jit(solution)/shard_map/tile/pallas_call | solution.py:700
  57.2 32.2 %sum_grads.1.gobs_ref.gkv_ref.gqo_ref = bf16[2,1152,512]{2,1,0:T(8,128)(2,1)} custom-call(bf16[2,1152,512]{2,1,0:T(8,128)(2,1)} %get-tuple-element.23.main_ref), custom_call_target="tpu_custom_call" | custom-call | tf_op jit(solution)/shard_map/sum_grads/pallas_call | solution.py:638
  89.3 4.3 %widen.1 = (f32[256,512]{1,0:T(8,128)}, f32[512,1024]{1,0:T(8,128)}, f32[512,512]{1,0:T(8,128)}, f32[512,512]{1,0:T(8,128)}) custom-call(bf16[2,1152,512]{2,1,0:T(8,128)(2,1)} %sum_grads.1.gobs_ref.gkv_ref.gqo_ref, bf16[2,1152,512]{2,1,0:T(8,128)(2,1)} %sum_grads.1.gobs_ref.gkv_ref.gqo_ref, bf16[2,1152,512]{2,1,0:T(8,128)(2,1)} %sum_grads.1.gobs_ref.gkv_ref.gqo_ref), custom_call_target="tpu_custom_call" | custom-call | tf_op jit(solution)/shard_map/widen/pallas_call | solution.py:740

commit v6 on v5

--- a/solution.py
+++ b/solution.py
@@ -64,9 +64,9 @@
 
 def exchange_kernel(
     foot_ref, obs_ref, bias_ref, cell_ref, lat_ref, dout_ref, wq_ref, wo_ref,
-    recv_ref, rmeta_ref, q_ref, back_ref,
+    recv_ref, place_ref, group_ref, q_ref, back_ref,
     foot_v, obs_v, bias_v, cell_v, lat_v, dout_v, wq_v, wo_v, q_v, back_v,
-    stage, mstage, osend, omsend, foot_s, marks_s, sem_in, sem_out, sem_core, sem_chip,
+    stage, mstage, rmeta, place_v, group_v, osend, omsend, foot_s, marks_s, sem_in, sem_out, sem_core, sem_chip,
 ):
     lat, lon = lax.axis_index("lat"), lax.axis_index("lon")
     core = lax.rem(lat, 2)
@@ -148,11 +148,12 @@
     for part in swap:
         part.wait_recv()
     for chip, where in chips:
+        copy(mstage.at[:, chip], rmeta.at[:, my_chip], sem_chip.at[2], where).start()
+    for chip, where in chips:
         copy(stage.at[1 - core, chip], recv_ref.at[1 - core, my_chip], sem_chip.at[1], where).start()
-        copy(mstage.at[:, chip], rmeta_ref.at[:, my_chip], sem_chip.at[2], where).start()
+    rmeta[:, my_chip] = mstage[:, my_chip]
     stores = [
         pltpu.make_async_copy(stage.at[:, my_chip], recv_ref.at[:, my_chip], sem_out.at[0]),
-        pltpu.make_async_copy(mstage.at[:, my_chip], rmeta_ref.at[:, my_chip], sem_out.at[1]),
     ]
     for store in stores:
         store.start()
@@ -171,35 +172,11 @@
     whole = [
         copy(stage.at[core, 0:63], recv_ref.at[core, 0:63], sem_chip.at[0], sibling),
         copy(stage.at[1 - core, 0:63], recv_ref.at[1 - core, 0:63], sem_chip.at[1], sibling),
-        copy(mstage.at[:, 0:63], rmeta_ref.at[:, 0:63], sem_chip.at[2], sibling),
+        copy(mstage.at[:, 0:63], rmeta.at[:, 0:63], sem_chip.at[2], sibling),
     ]
-    for part in whole:
-        part.wait_recv()
-    for part in whole:
-        part.wait_send()
-    for part in swap:
-        part.wait_send()
-    for store in stores:
-        store.wait()
-
-
-def tile_kernel(
-    recv_ref, rmeta_ref, q_ref, back_ref, lat_ref, dout_ref, wobs_ref, wkv_ref, wq_ref, wo_ref,
-    upd_ref, dlat_ref, main_ref,
-    rowst_s, slope_s, enct_s, kv_s, bias_s, attn_s, dq_s, dpre_s, sums_s, main_v, upd_v, dlat_v, meta_sm,
-    recv_v, rmeta_v, q_s, back_s, lat_v, dout_v, wobs_v, wkv_v, wq_v, wo_v, sem_in, sem_out,
-):
-    loads = []
-    for i, (src, dst) in enumerate((
-        (rmeta_ref, rmeta_v), (recv_ref, recv_v), (wobs_ref, wobs_v), (wkv_ref, wkv_v), (q_ref, q_s), (back_ref, back_s),
-        (lat_ref, lat_v), (dout_ref, dout_v), (wq_ref, wq_v), (wo_ref, wo_v),
-    )):
-        loads.append(pltpu.make_async_copy(src, dst, sem_in.at[i]))
-        loads[-1].start()
-
-    loads[0].wait()
+    whole[2].wait_recv()
     r, c = iota((128, 128), 0), iota((128, 128), 1)
-    marks = rmeta_v[...].astype(BF16)
+    marks = rmeta[...].reshape(DEV, 128).astype(BF16)
     own_lane = r % 8 == c // 16
     chunk = jnp.where(iota((16, 128), 0) == iota((16, 128), 1) // 8, 1.0, 0.0).astype(BF16)
 
@@ -222,10 +199,44 @@
     pos = place[0:16, :]
     for g in range(1, GROUPS):
         pos = jnp.maximum(pos, place[g * 16 : (g + 1) * 16, :])
+    place_v[0] = pos
+    place_v[1] = bias_row
+    for kind, values in enumerate((first, nblk, count)):
+        group_v[kind] = jnp.concatenate([values[g * 16 : g * 16 + 8, :] for g in range(GROUPS)], axis=0)
+    stores.append(pltpu.make_async_copy(place_v, place_ref, sem_out.at[1]))
+    stores[-1].start()
+    stores.append(pltpu.make_async_copy(group_v, group_ref, sem_out.at[4]))
+    stores[-1].start()
+    for part in whole[:2]:
+        part.wait_recv()
+    for part in whole:
+        part.wait_send()
+    for part in swap:
+        part.wait_send()
+    for store in stores:
+        store.wait()
+
+
+def tile_kernel(
+    recv_ref, place_ref, group_ref, q_ref, back_ref, lat_ref, dout_ref, wobs_ref, wkv_ref, wq_ref, wo_ref,
+    upd_ref, dlat_ref, main_ref,
+    rowst_s, slope_s, enct_s, kv_s, bias_s, attn_s, dq_s, dpre_s, sums_s, main_v, upd_v, dlat_v, meta_sm,
+    recv_v, place_v, group_v, q_s, back_s, lat_v, dout_v, wobs_v, wkv_v, wq_v, wo_v, sem_in, sem_out,
+):
+    loads = []
+    for i, (src, dst) in enumerate((
+        (group_ref, group_v), (place_ref, place_v), (recv_ref, recv_v), (wobs_ref, wobs_v), (wkv_ref, wkv_v), (q_ref, q_s), (back_ref, back_s),
+        (lat_ref, lat_v), (dout_ref, dout_v), (wq_ref, wq_v), (wo_ref, wo_v),
+    )):
+        loads.append(pltpu.make_async_copy(src, dst, sem_in.at[i]))
+        loads[-1].start()
+
+    loads[0].wait()
+    loads[1].wait()
+    pos, bias_row = place_v[0], place_v[1]
     for g in range(GROUPS):
-        meta_sm[0, g] = jnp.max(first[g * 16 : g * 16 + 8, :]).astype(jnp.int32)
-        meta_sm[1, g] = jnp.max(nblk[g * 16 : g * 16 + 8, :]).astype(jnp.int32)
-        meta_sm[2, g] = jnp.max(count[g * 16 : g * 16 + 8, :]).astype(jnp.int32)
+        for kind in range(3):
+            meta_sm[kind, g] = jnp.max(group_v[kind, g * 8 : g * 8 + 8, :]).astype(jnp.int32)
     blocks = meta_sm[0, GROUPS - 1] + meta_sm[1, GROUPS - 1]
 
     lane_pos = [jnp.broadcast_to(pos[i : i + 1, :], (16, 128)) for i in range(16)]
@@ -256,7 +267,7 @@
         enct_s[:, at] = enc.T
         kv_s[at, :] = dot(enc, wkv_v[...]).astype(BF16)
 
-    for load in loads[1:4]:
+    for load in loads[2:5]:
         load.wait()
     last = None
     for i in range(LEAD * KB // SPAN):
@@ -273,7 +284,7 @@
         return carry
 
     lax.fori_loop(LEAD, blocks, encode, 0)
-    for load in loads[4:6]:
+    for load in loads[5:7]:
         load.wait()
 
     lane_head = iota((GCELLS, 256), 1) // 64
@@ -404,7 +415,7 @@
 
     lax.fori_loop(0, GROUPS // 2, pair, 0)
 
-    for load in loads[6:]:
+    for load in loads[7:]:
         load.wait()
     attn, dq = attn_s[...], dq_s[...]
     outs = []
@@ -419,6 +430,7 @@
     put_out(dlat_v, dlat_ref)
     main_v[0, 0:512, :] = dot_tn(lat_v[...], dq).astype(BF16)
     main_v[1, 0:512, :] = dot_tn(attn, dout_v[...]).astype(BF16)
+    put_out(main_v.at[:, 0:512, :], main_ref.at[:, 0:512, :])
 
     def through_encoder(at):
         return (dot_nt(kv_s[at, :], wkv_v[...]) * slope_s[at, :]).astype(BF16)
@@ -456,7 +468,7 @@
             main_v[h, 512:1024, :] = sums_s[0:512, h * 512 : (h + 1) * 512].astype(BF16)
             main_v[h, 1024:1152, :] = sums_s[512 + h * 128 : 640 + h * 128, 0:512].astype(BF16)
 
-    put_out(main_v, main_ref)
+    put_out(main_v.at[:, 512:HALF, :], main_ref.at[:, 512:HALF, :])
     for out in outs:
         out.wait()
 
@@ -657,16 +669,17 @@
     vmem = pl.BlockSpec(memory_space=pltpu.VMEM)
     dma = pltpu.SemaphoreType.DMA
     far = pl.BlockSpec(memory_space=pltpu.HBM)
-    recv, rmeta, q, back = pl.pallas_call(
+    recv, place, group, q, back = pl.pallas_call(
         exchange_kernel,
         out_shape=(
             jax.ShapeDtypeStruct((2, 64, 16, CH), BF16),
-            jax.ShapeDtypeStruct((2, 64, 1, 128), F32),
+            jax.ShapeDtypeStruct((2, 16, 128), F32),
+            jax.ShapeDtypeStruct((3, 64, 128), F32),
             jax.ShapeDtypeStruct((CELLS, D), BF16),
             jax.ShapeDtypeStruct((CELLS, D), BF16),
         ),
         in_specs=[far] * 8,
-        out_specs=[far] * 4,
+        out_specs=[far] * 5,
         scratch_shapes=[
             pltpu.VMEM((4, 32), jnp.int32),
             pltpu.VMEM((32 * OBS, CH), BF16),
@@ -680,12 +693,15 @@
             pltpu.VMEM((CELLS, D), BF16),
             pltpu.VMEM((2, 64, 16, CH), BF16),
             pltpu.VMEM((2, 64, 1, 128), F32),
+            pltpu.VMEM((2, 64, 1, 128), F32),
+            pltpu.VMEM((2, 16, 128), F32),
+            pltpu.VMEM((3, 64, 128), F32),
             pltpu.VMEM((64, 16, CH), BF16),
             pltpu.VMEM((64, 1, 128), F32),
             pltpu.VMEM((16, 128), F32),
             pltpu.VMEM((128, 1280), F32),
             dma((8,)),
-            dma((4,)),
+            dma((5,)),
             dma((2, 2)),
             dma((3, 2)),
         ],
@@ -704,7 +720,7 @@
             jax.ShapeDtypeStruct((CELLS, D), BF16),
             jax.ShapeDtypeStruct((2, HALF, D), BF16),
         ),
-        in_specs=[far] * 10,
+        in_specs=[far] * 11,
         out_specs=[far] * 3,
         scratch_shapes=[
             pltpu.VMEM((CH, MAXB * KB), BF16),
@@ -721,7 +737,8 @@
             pltpu.VMEM((CELLS, D), BF16),
             pltpu.SMEM((3, GROUPS), jnp.int32),
             pltpu.VMEM((ROWS, CH), BF16),
-            pltpu.VMEM((DEV, 128), F32),
+            pltpu.VMEM((2, 16, 128), F32),
+            pltpu.VMEM((3, 64, 128), F32),
             pltpu.VMEM((CELLS, D), BF16),
             pltpu.VMEM((CELLS, D), BF16),
             pltpu.VMEM((CELLS, D), BF16),
@@ -730,12 +747,12 @@
             pltpu.VMEM((D, 2 * D), BF16),
             pltpu.VMEM((D, D), BF16),
             pltpu.VMEM((D, D), BF16),
-            dma((10,)),
-            dma((3,)),
+            dma((11,)),
+            dma((4,)),
         ],
         compiler_params=pltpu.CompilerParams(vmem_limit_bytes=VMEM_LIMIT),
         name="tile",
-    )(recv.reshape(ROWS, CH), rmeta.reshape(DEV, 128), q, back, latents, d_out, w_obs, w_kv, w_q, w_o)
+    )(recv.reshape(ROWS, CH), place, group, q, back, latents, d_out, w_obs, w_kv, w_q, w_o)
     total = sum_grads(main)
     gobs, gkv, gq, go = pl.pallas_call(
         widen_kernel,

time: 93.9 us -> 93.2 us (level)
    pallas_call x1, Pallas kernels: 32.2 us -> 30.4 us  [sum_grads(): pl.pallas_call(sum_kernel, out_shape=jax.ShapeDtypeStruct((2, HALF, D), B...]
    pallas_call x1, Pallas kernels: 32.3 us -> 33.3 us  [body(): pl.pallas_call(tile_kernel, out_shape=(jax.ShapeDtypeStruct((CELLS, D), B...]
where the time goes in v6:
time: 93.2 us; the launch traced here: 92.8 us
  Pallas kernels  92.1 us (99%)
    pallas_call x1, Pallas kernels, body(): pl.pallas_call(tile_kernel, out_shape=(jax.ShapeDtypeStruct((CELLS, D), B...  33.3 us
    pallas_call x1, Pallas kernels, sum_grads(): pl.pallas_call(sum_kernel, out_shape=jax.ShapeDtypeStruct((2, HALF, D), B...  30.4 us
    pallas_call x1, Pallas kernels, body(): pl.pallas_call(exchange_kernel, out_shape=(jax.ShapeDtypeStruct((2, 64, 1...  24.2 us
    pallas_call x1, Pallas kernels, body(): pl.pallas_call(widen_kernel, grid=(4,), out_shape=[jax.ShapeDtypeStruct(x...  4.33 us

profile of v6, /device:TPU:1, one launch (start us, length us, event | category | flops | bytes accessed | tf_op | source)
XLA Modules:
  0.0 92.8 jit_solution(27532347503191441)
XLA Ops:
  0.6 24.2 %exchange.1 = (bf16[2,64,16,256]{3,2,1,0:T(8,128)(2,1)}, f32[2,16,128]{2,1,0:T(8,128)}, f32[3,64,128]{2,1,0:T(8,128)}, bf16[1024,512]{1,0:T(8,128)(2,1)}, bf16[1024,512]{1,0:T(8,128)(2,1)}) custom-call(s32[4,32]{1,0:T(4,128)} %bitcast.8, bf16[256,256]{1,0:T(8,128)(2,1)} %bitcast.6, bf16[8,32]{1,0:T(8,128)(2,1)} %bitcast.9, s32[4,8,32]{2,1,0:T(8,128)} %bitcast.7, ...), custom_call_target="tpu_custom_call" | custom-call | tf_op jit(solution)/shard_map/exchange/pallas_call | solution.py:672
  24.8 33.3 %tile.1 = (bf16[1024,512]{1,0:T(8,128)(2,1)}, bf16[1024,512]{1,0:T(8,128)(2,1)}, bf16[2,1152,512]{2,1,0:T(8,128)(2,1)}) custom-call(bf16[2048,256]{1,0:T(8,128)(2,1)} %bitcast.5, f32[2,16,128]{2,1,0:T(8,128)} %get-tuple-element.19.place_ref, f32[3,64,128]{2,1,0:T(8,128)} %get-tuple-element.20.group_ref, bf16[1024,512]{1,0:T(8,128)(2,1)} %get-tuple-element.21.q_ref, ...), custom_call_target="tpu_custom_call" | custom-call | tf_op jit(solution)/shard_map/tile/pallas_call | solution.py:716
  58.1 30.4 %sum_grads.1.gobs_ref.gkv_ref.gqo_ref = bf16[2,1152,512]{2,1,0:T(8,128)(2,1)} custom-call(bf16[2,1152,512]{2,1,0:T(8,128)(2,1)} %get-tuple-element.25.main_ref), custom_call_target="tpu_custom_call" | custom-call | tf_op jit(solution)/shard_map/sum_grads/pallas_call | solution.py:650
  88.5 4.3 %widen.1 = (f32[256,512]{1,0:T(8,128)}, f32[512,1024]{1,0:T(8,128)}, f32[512,512]{1,0:T(8,128)}, f32[512,512]{1,0:T(8,128)}) custom-call(bf16[2,1152,512]{2,1,0:T(8,128)(2,1)} %sum_grads.1.gobs_ref.gkv_ref.gqo_ref, bf16[2,1152,512]{2,1,0:T(8,128)(2,1)} %sum_grads.1.gobs_ref.gkv_ref.gqo_ref, bf16[2,1152,512]{2,1,0:T(8,128)(2,1)} %sum_grads.1.gobs_ref.gkv_ref.gqo_ref), custom_call_target="tpu_custom_call" | custom-call | tf_op jit(solution)/shard_map/widen/pallas_call | solution.py:757
